TPU v7x, 128 devices: a whole 4x4x4 slice. The times are simulated.
128 devices in a mesh: grid: 32 (over x, z, core), row: 4 (over y).
Axes of the slice: x: 4, y: 4, z: 4, core: 2. Of those that a mesh axis runs over, the one named last changes fastest.
Arguments:
- first_block: bfloat16 [16, 2048, 2048], P('row', 'grid'), may hold values from -6 to 6
- second_block: bfloat16 [16, 2048, 2048], P('row', 'grid'), may hold values from -6 to 6
- spectrum: float32 [2048, 2048], P('grid'), may hold values from 0.07 to 17, as said below
- first_ids: int32 [16], P('row'), may hold values from 0 to 2047
- second_ids: int32 [16], replicated, may hold values from 0 to 2047
- error_scale: float32 [2048], replicated, may hold values from 0.5 to 2
Outputs:
- whitened: float32 [16, 16], P('row')
Inputs may be any that keep to these rules, and one draw needn't show every extreme that they name: Every entry is positive, and spectrum[ky, kx] equals spectrum[(2048 - ky) % 2048, (2048 - kx) % 2048].
All inputs are finite; a program needn't handle non-finite values.
Results may differ from a plain program's by a relative error of at most 0.009.
Values may be sent and summed in bfloat16 or wider, within the bound.
No kernel may reach another device: no remote copies, remote signals or barrier semaphores. Data moves between devices by JAX's collectives and lax.ppermute only.
A program may use at most 128 MiB of HBM per device.

v0:
```python
import math

import jax
import jax.numpy as jnp
from jax import lax
from jax.sharding import PartitionSpec as P


def tables(length):
    index_row = jnp.arange(length, dtype=jnp.int32)
    product = index_row[:, None] * index_row[None, :] % length
    theta = product.astype(jnp.float32) * (2.0 * math.pi / length)
    return (jnp.cos(theta).astype(jnp.bfloat16), jnp.sin(theta).astype(jnp.bfloat16))


def lookup(indices, table):
    onehot = (indices[:, None] == jnp.arange(table.shape[0], dtype=jnp.int32)[None, :]).astype(
        jnp.float32
    )
    return jnp.dot(onehot, table, precision=lax.Precision.HIGHEST)


def shards(first_block, second_block, spectrum, first_ids, second_ids, error_scale):
    wide = jnp.float32
    groups = lax.axis_size("grid")
    row_count, slab_width, length = first_block.shape
    cosine, sine = tables(length)
    real_part = jnp.einsum("rxy,yk->krx", first_block, cosine, preferred_element_type=wide).astype(
        jnp.bfloat16
    )
    imag_part = (-jnp.einsum("rxy,yk->krx", first_block, sine, preferred_element_type=wide)).astype(
        jnp.bfloat16
    )
    real_part = real_part.reshape(length, row_count * slab_width)
    imag_part = imag_part.reshape(length, row_count * slab_width)
    real_part, imag_part = (
        lax.all_to_all(real_part, "grid", split_axis=0, concat_axis=1, tiled=True),
        lax.all_to_all(imag_part, "grid", split_axis=0, concat_axis=1, tiled=True),
    )
    band_rows = real_part.shape[0]
    real_blocks = real_part.reshape(band_rows, groups, row_count, slab_width)
    imag_blocks = imag_part.reshape(band_rows, groups, row_count, slab_width)
    cos_blocks = cosine.reshape(groups, slab_width, length)
    sin_blocks = sine.reshape(groups, slab_width, length)
    spec_real = jnp.einsum(
        "kprx,pxm->krm", real_blocks, cos_blocks, preferred_element_type=wide
    ) + jnp.einsum("kprx,pxm->krm", imag_blocks, sin_blocks, preferred_element_type=wide)
    spec_imag = jnp.einsum(
        "kprx,pxm->krm", imag_blocks, cos_blocks, preferred_element_type=wide
    ) - jnp.einsum("kprx,pxm->krm", real_blocks, sin_blocks, preferred_element_type=wide)
    factor = (spectrum / (length * length))[:, None, :]
    scaled_real = (spec_real * factor).astype(jnp.bfloat16)
    scaled_imag = (spec_imag * factor).astype(jnp.bfloat16)
    cos_back = cosine.reshape(length, groups, slab_width)
    sin_back = sine.reshape(length, groups, slab_width)
    back_real = (
        jnp.einsum("krm,mpx->kprx", scaled_real, cos_back, preferred_element_type=wide)
        - jnp.einsum("krm,mpx->kprx", scaled_imag, sin_back, preferred_element_type=wide)
    ).astype(jnp.bfloat16)
    back_imag = (
        jnp.einsum("krm,mpx->kprx", scaled_imag, cos_back, preferred_element_type=wide)
        + jnp.einsum("krm,mpx->kprx", scaled_real, sin_back, preferred_element_type=wide)
    ).astype(jnp.bfloat16)
    back_real = back_real.reshape(band_rows, groups * row_count * slab_width)
    back_imag = back_imag.reshape(band_rows, groups * row_count * slab_width)
    back_real, back_imag = (
        lax.all_to_all(back_real, "grid", split_axis=1, concat_axis=0, tiled=True),
        lax.all_to_all(back_imag, "grid", split_axis=1, concat_axis=0, tiled=True),
    )
    field_rows = jnp.dot(cosine, back_real, preferred_element_type=wide) - jnp.dot(
        sine, back_imag, preferred_element_type=wide
    )
    covaried = field_rows.astype(jnp.bfloat16)
    covaried_rows = covaried.reshape(length, row_count, slab_width)
    partial_value = jnp.einsum(
        "yrx,jxy->rj",
        covaried_rows,
        lax.all_gather(second_block, "row", axis=0, tiled=True),
        preferred_element_type=jnp.float32,
    )
    cross_block = lax.psum(partial_value, "grid")
    scale_first = lookup(first_ids, error_scale)
    scale_second = lookup(second_ids, error_scale)
    return cross_block / (length * scale_first[:, None] * scale_second[None, :])


def solution(mesh):
    return jax.shard_map(
        shards,
        mesh=mesh,
        in_specs=(
            P("row", "grid", None),
            P("row", "grid", None),
            P("grid", None),
            P("row"),
            P(),
            P(),
        ),
        out_specs=P("row", None),
        check_vma=False,
    )
```

profile of v0, /device:TPU:1, one launch (start us, length us, event | category | flops | bytes accessed | tf_op | source)
XLA Modules:
  0.0 924.1 jit_solution(8240071365808966779)
XLA Ops:
  7.8 63.9 %fusion.84 = bf16[2048,4,64]{0,2,1:T(8,128)(2,1)} fusion(bf16[4,64,2048]{2,1,0:T(8,128)(2,1)S(1)} %copy-done), kind=kOutput, calls=%fused_computation.69 | convolution fusion | flops 2210922496 | bytes 2097152 | tf_op jit(solution)/shard_map/rxy,yk->krx/dot_general | solution.py:28
  71.6 3.3 all_to_all.52
  75.0 2.5 copy.19
  77.5 9.9 %all-to-all-start = ((bf16[32,64,256]{2,1,0:T(8,128)(2,1)}), bf16[32,64,256]{2,1,0:T(8,128)(2,1)}, u32[]{:S(2)}, u32[]{:S(2)}) async-start(bf16[32,64,256]{2,1,0:T(8,128)(2,1)} %copy.19), calls=%async_computation | async-start | bytes 2097152 | tf_op jit(solution)/shard_map/all_to_all | solution.py:37
  87.4 64.3 %fusion.81 = bf16[2048,4,64]{0,2,1:T(8,128)(2,1)} fusion(bf16[4,64,2048]{2,1,0:T(8,128)(2,1)S(1)} %copy-done), kind=kOutput, calls=%fused_computation.68 | convolution fusion | flops 2211446784 | bytes 2097152 | tf_op jit(solution)/shard_map/rxy,yk->krx/dot_general | solution.py:31
  151.7 3.4 all_to_all.55
  155.1 2.5 copy.22
  157.6 7.4 all-to-all-start.1
  168.4 4.4 reshape.178
  172.9 9.0 all-to-all-done.1
  183.8 65.5 %fusion.46 = f32[64,4,2048]{2,0,1:T(8,128)S(1)} fusion(s32[32,64]{1,0:T(8,128)S(1)} %multiply_add_fusion, bf16[64,32,4,64]{3,2,0,1:T(4,128)(2,1)} %reshape.178), kind=kOutput, calls=%fused_computation.55 | convolution fusion | flops 2210398208 | bytes 3153920 | tf_op jit(solution)/shard_map/kprx,pxm->krm/dot_general | solution.py:45
  249.3 64.5 %fusion.49 = f32[64,4,2048]{2,0,1:T(8,128)S(1)} fusion(s32[32,64]{1,0:T(8,128)S(1)} %multiply_add_fusion, bf16[64,32,4,64]{3,2,0,1:T(4,128)(2,1)S(1)} %copy-done.2), kind=kOutput, calls=%fused_computation.56 | convolution fusion | flops 2210398208 | bytes 3153920 | tf_op jit(solution)/shard_map/kprx,pxm->krm/dot_general | solution.py:48
  313.9 64.9 %fusion.87 = bf16[64,4,2048,1]{2,0,1,3:T(8,128)(2,1)S(1)} fusion(f32[64,4,2048]{2,0,1:T(8,128)S(1)} %fusion.46, s32[32,64]{1,0:T(8,128)S(1)} %multiply_add_fusion, bf16[64,32,4,64]{3,2,0,1:T(4,128)(2,1)S(1)} %copy-done.2, f32[64,2048]{1,0:T(8,128)S(1)} %broadcast_multiply_fusion), kind=kOutput, calls=%fused_computation.70 | convolution fusion | flops 2211971072 | bytes 4726784 | tf_op jit(solution)/shard_map/kprx,pxm->krm/dot_general | solution.py:47
  378.8 65.0 %fusion.34 = f32[32,64,64,4]{2,1,3,0:T(8,128)} fusion(bf16[64,4,2048,1]{2,0,1,3:T(8,128)(2,1)S(1)} %fusion.87, s32[32,64]{1,0:T(8,128)S(1)} %multiply_add_fusion), kind=kOutput, calls=%fused_computation.45 | convolution fusion | flops 2210398208 | bytes 3153920 | tf_op jit(solution)/shard_map/krm,mpx->kprx/dot_general | solution.py:62
  443.8 64.9 %fusion.90 = bf16[64,4,2048,1]{2,0,1,3:T(8,128)(2,1)S(1)} fusion(f32[64,4,2048]{2,0,1:T(8,128)S(1)} %fusion.49, s32[32,64]{1,0:T(8,128)S(1)} %multiply_add_fusion, bf16[64,32,4,64]{3,2,0,1:T(4,128)(2,1)S(1)} %copy-done.1, f32[64,2048]{1,0:T(8,128)S(1)} %broadcast_multiply_fusion), kind=kOutput, calls=%fused_computation.71 | convolution fusion | flops 2211971072 | bytes 4726784 | tf_op jit(solution)/shard_map/kprx,pxm->krm/dot_general | solution.py:50
  508.7 63.8 %fusion.36 = f32[32,64,64,4]{2,1,3,0:T(8,128)S(1)} fusion(bf16[64,4,2048,1]{2,0,1,3:T(8,128)(2,1)S(1)} %fusion.90, s32[32,64]{1,0:T(8,128)S(1)} %multiply_add_fusion), kind=kOutput, calls=%fused_computation.46 | convolution fusion | flops 2210398208 | bytes 3153920 | tf_op jit(solution)/shard_map/krm,mpx->kprx/dot_general | solution.py:58
  572.5 62.8 %subtract_convert_fusion = bf16[32,64,64,4]{2,1,3,0:T(8,128)(2,1)S(1)} fusion(f32[32,64,64,4]{2,1,3,0:T(8,128)S(1)} %fusion.36, bf16[64,4,2048,1]{2,0,1,3:T(8,128)(2,1)S(1)} %fusion.87, s32[32,64]{1,0:T(8,128)S(1)} %multiply_add_fusion), kind=kOutput, calls=%fused_computation.54 | convolution fusion | flops 2211446784 | bytes 4202496 | tf_op jit(solution)/shard_map/krm,mpx->kprx/dot_general | solution.py:57
  636.9 4.4 all-to-all-start.2
  641.4 64.9 %add_convert_fusion = bf16[32,64,64,4]{2,1,3,0:T(8,128)(2,1)S(1)} fusion(f32[32,64,64,4]{2,1,3,0:T(8,128)} %fusion.34, bf16[64,4,2048,1]{2,0,1,3:T(8,128)(2,1)} %copy-done.8, s32[32,64]{1,0:T(8,128)S(1)} %multiply_add_fusion), kind=kOutput, calls=%fused_computation.53 | convolution fusion | flops 2211446784 | bytes 4202496 | tf_op jit(solution)/shard_map/krm,mpx->kprx/dot_general | solution.py:61
  707.9 7.4 all-to-all-start.3
  715.3 64.3 %fusion.42 = f32[2048,256]{0,1:T(8,128)} fusion(bf16[2048,256]{1,0:T(8,128)(2,1)} %bitcast.25), kind=kOutput, calls=%fused_computation.49 | convolution fusion | flops 2210398208 | bytes 3145728 | tf_op jit(solution)/shard_map/dot_general | solution.py:70
  779.7 66.1 %fusion.80 = bf16[2048,256]{0,1:T(8,128)(2,1)S(1)} fusion(f32[2048,256]{0,1:T(8,128)} %fusion.42, bf16[2048,256]{1,0:T(8,128)(2,1)S(1)} %bitcast.168), kind=kOutput, calls=%fused_computation.67 | convolution fusion | flops 2211446784 | bytes 4194304 | tf_op jit(solution)/shard_map/dot_general | solution.py:70
  845.8 7.8 fusion.101
  853.6 62.5 %psum.7 = f32[4,16]{1,0:T(4,128)S(1)} all-reduce(f32[4,16]{1,0:T(4,128)S(1)} %fusion.101), channel_id=1, replica_groups=mesh['grid'=32,'row'=4] {'grid'}, use_global_device_ids=true, to_apply=%region_0.1 | all-reduce | flops 64 | bytes 512 | tf_op jit(solution)/shard_map/psum | solution.py:81
  (32 shorter events, 10.4 us)
Async XLA Ops:
  6.5 1.2 copy-start
  77.5 80.1 %all-to-all-start = ((bf16[32,64,256]{2,1,0:T(8,128)(2,1)}), bf16[32,64,256]{2,1,0:T(8,128)(2,1)}, u32[]{:S(2)}, u32[]{:S(2)}) async-start(bf16[32,64,256]{2,1,0:T(8,128)(2,1)} %copy.19), calls=%async_computation | async-start | bytes 2097152 | tf_op jit(solution)/shard_map/all_to_all | solution.py:37
  151.7 14.0 %copy-start.5 = (f32[2048]{0:T(1024)S(1)}, f32[2048]{0:T(1024)}, u32[]{:S(2)}) copy-start(f32[2048]{0:T(1024)} %param.11) | copy-start | bytes 24580
  151.7 14.1 %copy-start.6 = (s32[16]{0:T(128)S(1)}, s32[16]{0:T(128)}, u32[]{:S(2)}) copy-start(s32[16]{0:T(128)} %param.10) | copy-start | bytes 196
  151.7 14.8 %copy-start.7 = (s32[4]{0:T(128)S(1)}, s32[4]{0:T(128)}, u32[]{:S(2)}) copy-start(s32[4]{0:T(128)} %param.9) | copy-start | bytes 52
  157.6 24.3 %all-to-all-start.1 = ((bf16[32,64,256]{2,1,0:T(8,128)(2,1)}), bf16[32,64,256]{2,1,0:T(8,128)(2,1)S(1)}, u32[]{:S(2)}, u32[]{:S(2)}) async-start(bf16[32,64,256]{2,1,0:T(8,128)(2,1)} %copy.22), calls=%async_computation.1 | async-start | bytes 2097152 | tf_op jit(solution)/shard_map/all_to_all | solution.py:38
  165.0 680.8 %all-gather.2.cloned.1.call-start = ((), (), s32[]{:S(2)}) async-start(), calls=%async_computation.4 | async-start | bytes 5242880 | tf_op jit(solution)/shard_map/all_gather | solution.py:78
  183.8 65.6 %copy-start.2 = (bf16[64,32,4,64]{3,2,0,1:T(4,128)(2,1)S(1)}, bf16[64,32,4,64]{3,2,0,1:T(4,128)(2,1)}, u32[]{:S(2)}) copy-start(bf16[64,32,4,64]{3,2,0,1:T(4,128)(2,1)} %reshape.179) | copy-start | bytes 3145732
  378.8 65.0 %copy-start.1 = (bf16[64,32,4,64]{3,2,0,1:T(4,128)(2,1)S(1)}, bf16[64,32,4,64]{3,2,0,1:T(4,128)(2,1)}, u32[]{:S(2)}) copy-start(bf16[64,32,4,64]{3,2,0,1:T(4,128)(2,1)} %reshape.178) | copy-start | bytes 3145732
  508.7 63.8 %copy-start.8 = (bf16[64,4,2048,1]{2,0,1,3:T(8,128)(2,1)}, bf16[64,4,2048,1]{2,0,1,3:T(8,128)(2,1)S(1)}, u32[]{:S(2)}) copy-start(bf16[64,4,2048,1]{2,0,1,3:T(8,128)(2,1)S(1)} %fusion.90) | copy-start | bytes 3145732
  636.9 71.0 %all-to-all-start.2 = ((bf16[64,32,256]{2,0,1:T(8,128)(2,1)}), bf16[64,32,256]{2,0,1:T(8,128)(2,1)}, u32[]{:S(2)}, u32[]{:S(2)}) async-start(bf16[64,32,256]{2,0,1:T(8,128)(2,1)} %copy.27), calls=%async_computation.2 | async-start | bytes 2097152 | tf_op jit(solution)/shard_map/all_to_all | solution.py:67
  707.9 71.8 %all-to-all-start.3 = ((bf16[64,32,256]{2,0,1:T(8,128)(2,1)}), bf16[64,32,256]{2,0,1:T(8,128)(2,1)S(1)}, u32[]{:S(2)}, u32[]{:S(2)}) async-start(bf16[64,32,256]{2,0,1:T(8,128)(2,1)} %copy.28), calls=%async_computation.3 | async-start | bytes 2097152 | tf_op jit(solution)/shard_map/all_to_all | solution.py:68
  845.8 70.4 %copy-start.3 = (f32[16]{0:T(128)S(1)}, f32[16]{0:T(128)}, u32[]{:S(2)}) copy-start(f32[16]{0:T(128)} %convolution_bitcast_fusion) | copy-start | bytes 196
  845.8 70.4 %copy-start.4 = (f32[4]{0:T(128)S(1)}, f32[4]{0:T(128)}, u32[]{:S(2)}) copy-start(f32[4]{0:T(128)} %fusion.104) | copy-start | bytes 52
Sparse Core Ops, SparseCore 0:
  167.5 49.4 all-gather.1
where the time goes:
time: 937 us; the launch traced here: 924 us
  matrix products  784 us (84%)
  blocking collectives  62.5 us (7%)
  starting transfers between devices  29.6 us (3%)
  local copies, waits for them, and re-layouts  22.5 us (2%)
  between operations  14.1 us (2%)
    dot_general x1, matrix products, shards(): jnp.dot(sine, back_imag, preferred_element_type=wide)  66.1 us
    dot_general x1, matrix products, shards(): jnp.einsum('kprx,pxm->krm', real_blocks, cos_blocks, preferred_element_ty...  65.5 us
    dot_general x1, matrix products, shards(): jnp.einsum('krm,mpx->kprx', scaled_real, sin_back, preferred_element_type...  65 us
    dot_general x1, matrix products, shards(): jnp.einsum('kprx,pxm->krm', real_blocks, sin_blocks, preferred_element_ty...  64.9 us
    dot_general x1, matrix products, shards(): jnp.einsum('kprx,pxm->krm', imag_blocks, sin_blocks, preferred_element_ty...  64.9 us
    dot_general x1, matrix products, shards(): jnp.einsum('krm,mpx->kprx', scaled_imag, cos_back, preferred_element_type...  64.9 us
    dot_general x1, matrix products, shards(): jnp.einsum('kprx,pxm->krm', imag_blocks, cos_blocks, preferred_element_ty...  64.5 us
    dot_general x1, matrix products, shards(): jnp.dot(cosine, back_real, preferred_element_type=wide)  64.3 us
  transfers between devices with their start and end apart: 5, of which 1 were waited for; matrix products, arithmetic and copies ran while one was open for 79% of the time, Pallas kernels for 0%

commit v1 on v0

v1 whole, which is shorter than its diff:
```python
import functools
import math

import jax
import jax.numpy as jnp
import ml_dtypes
import numpy as np
from jax import lax
from jax.experimental import pallas as pl
from jax.experimental.pallas import tpu as pltpu
from jax.sharding import PartitionSpec as P

N = 2048
SLABS = 32
GROUPS = 4
CELLS = N // SLABS
ROWS = 4
WAVES = 8
LANES = ROWS * CELLS
EVERY = ("grid", "row")

NT = (((1,), (1,)), ((), ()))


def rounded(array):
    return np.asarray(array, np.float64).astype(ml_dtypes.bfloat16)


def offsets(kind, j):
    return (4 * j, 4 * j + 2, 8 * (j // 2) + 1 + 6 * (j % 2), 8 * (j // 2) + 5 - 2 * (j % 2))[kind]


@functools.lru_cache(None)
def make_tables():
    y = np.arange(N // 4)
    j = np.arange(WAVES)
    half = np.zeros((4, SLABS // 2, 2, 2, WAVES, N // 4))
    for kind in range(4):
        for low in range(2):
            for slab in range(SLABS // 2):
                waves = CELLS * (slab + SLABS // 2 * (kind // 2)) + 32 * low + offsets(kind, j)
                if kind < 2:
                    angle = 2 * np.pi * ((waves[:, None] * y[None, :]) % N) / N
                    half[kind, slab, low, 0] = np.cos(angle)
                    half[kind, slab, low, 1] = -np.sin(angle)
                    continue
                mirror = waves % 8 != (1 if kind == 2 else 5)
                waves = np.where(mirror, N - waves, waves)
                angle = 2 * np.pi * ((waves[:, None] * y[None, : N // 8]) % N) / N
                sign = np.where(mirror, -1, 1)[:, None]
                half[kind, slab, low, 0] = np.concatenate([np.cos(angle), np.sin(angle)], 1)
                half[kind, slab, low, 1] = sign * np.concatenate([-np.sin(angle), np.cos(angle)], 1)
    half[0, 0, 0, 1, 0] = (-1.0) ** y
    half = rounded(half.reshape(N, N // 4))
    q = np.arange(SLABS)
    angle = 2 * np.pi * ((q[:, None] * q[None, :]) % SLABS) / SLABS
    cos, sin = np.cos(angle), np.sin(angle)
    outer = np.zeros((WAVES, 2, SLABS, SLABS, 2, WAVES))
    for k in range(WAVES):
        outer[k, 0, :, :, 0, k] = cos
        outer[k, 0, :, :, 1, k] = sin
        outer[k, 1, :, :, 1, k] = cos
        outer[k, 1, :, :, 0, k] = -sin
    outer = rounded(outer.reshape(WAVES * 2 * SLABS, -1))
    x = np.arange(CELLS)
    angle = 2 * np.pi * (q[:, None] * x[None, :]) / N
    twist = np.stack([np.tile(np.cos(angle), (1, 2)), np.tile(np.sin(angle), (1, 2))]).astype(np.float32)
    angle = 2 * np.pi * ((x[:, None] * x[None, :]) % CELLS) / CELLS
    cos, sin = np.cos(angle), np.sin(angle)
    inner = np.stack([np.stack([cos, sin], 1), np.stack([-sin, cos], 1)])
    inner = inner.reshape(2, CELLS // 4, 4, 1, 2, 1, CELLS).transpose(0, 2, 3, 1, 4, 5, 6)
    inner = np.broadcast_to(inner, (2, 4, ROWS, CELLS // 4, 2, 2, CELLS))
    inner = rounded(inner.reshape(2 * LANES, LANES))
    return half, outer, twist, inner


PIECES = 4


def half_kernel(a_hbm, b_hbm, table_hbm, out_hbm, block_ref, table_ref, fold_ref, out_ref, block_sem, table_sem, out_sem):
    rows, width = N // PIECES, N // 4
    blocks = [
        pltpu.make_async_copy(hbm, block_ref.at[place], block_sem.at[place]) for place, hbm in enumerate((a_hbm, b_hbm))
    ]
    pieces = [
        pltpu.make_async_copy(
            table_hbm.at[pl.ds(rows * p, rows)], table_ref.at[pl.ds(rows * p, rows)], table_sem.at[p]
        )
        for p in range(PIECES)
    ]
    for copy in blocks + pieces:
        copy.start()
    for place, copy in enumerate(blocks):
        copy.wait()
        own = pl.ds(LANES * place, LANES)
        for side in range(2):
            first, second, third, fourth = (
                block_ref[place, :, pl.ds(width * p + width // 2 * side, width // 2)].astype(jnp.float32)
                for p in range(4)
            )
            even, odd = first + third, second + fourth
            lanes = pl.ds(width // 2 * side, width // 2)
            fold_ref[0, own, lanes] = (even + odd).astype(jnp.bfloat16)
            fold_ref[1, own, lanes] = (even - odd).astype(jnp.bfloat16)
            even, odd = first - third, second - fourth
            if side == 0:
                real, imag = even, -odd
            else:
                turn_real, turn_imag = (even - odd) * math.sqrt(0.5), (even + odd) * -math.sqrt(0.5)
        for kind, sign in ((2, 1.0), (3, -1.0)):
            fold_ref[kind, own, : width // 2] = (real + sign * turn_real).astype(jnp.bfloat16)
            fold_ref[kind, own, width // 2 :] = (imag + sign * turn_imag).astype(jnp.bfloat16)
    sends = []
    for p, copy in enumerate(pieces):
        copy.wait()
        value = lax.dot_general(
            table_ref[pl.ds(rows * p, rows), :], fold_ref[p], NT, preferred_element_type=jnp.float32
        )
        chunks = pl.ds(SLABS // 2 * (p // 2), SLABS // 2), pl.ds(2 * (p % 2), 2)
        out_ref[p] = value.astype(jnp.bfloat16).reshape(SLABS // 2, 2, 16, 2 * LANES)
        send = pltpu.make_async_copy(out_ref.at[p], out_hbm.at[chunks], out_sem.at[p])
        send.start()
        sends.append(send)
    for send in sends:
        send.wait()


def half_transform(first, second, table):
    return pl.pallas_call(
        half_kernel,
        in_specs=[pl.BlockSpec(memory_space=pl.ANY)] * 3,
        out_specs=pl.BlockSpec(memory_space=pl.ANY),
        out_shape=jax.ShapeDtypeStruct((SLABS, GROUPS, 16, 2 * LANES), jnp.bfloat16),
        scratch_shapes=[
            pltpu.VMEM((2, LANES, N), jnp.bfloat16),
            pltpu.VMEM((N, N // 4), jnp.bfloat16),
            pltpu.VMEM((4, 2 * LANES, N // 4), jnp.bfloat16),
            pltpu.VMEM((PIECES, SLABS // 2, 2, 16, 2 * LANES), jnp.bfloat16),
            pltpu.SemaphoreType.DMA((2,)),
            pltpu.SemaphoreType.DMA((PIECES,)),
            pltpu.SemaphoreType.DMA((PIECES,)),
        ],
        compiler_params=pltpu.CompilerParams(vmem_limit_bytes=60 * 2**20),
        cost_estimate=pl.CostEstimate(flops=N * 1024 * 512, bytes_accessed=6 * 2**20, transcendentals=0),
    )(first, second, table)


def turned(value, amount):
    amount = (SLABS * amount) % 128
    return pltpu.roll(value, amount, 1) if amount else value


def weight_kernel(spectrum_ref, nyquist_ref, weight_ref, shift_ref):
    slab, group = lax.axis_index("grid"), lax.axis_index("row")
    own = spectrum_ref[pl.ds(pl.multiple_of(32 * (group % 2), 32), 32), :]
    own = jnp.concatenate([own, jnp.broadcast_to(nyquist_ref[...], (8, N))], axis=0)
    own = jnp.concatenate([own[:, 128 * c : 128 * (c + 1)] for c in range(16)], axis=0)
    kind = 2 * (slab // (SLABS // 2)) + group // 2
    shape = ((WAVES + 1) * 16, 16 * 40)
    below, along = lax.broadcasted_iota(jnp.int32, (shape[0], 1), 0), lax.broadcasted_iota(jnp.int32, shape, 1)
    wave, coarse = below // 16, below % 16
    wanted = jnp.zeros_like(wave)
    for each in range(4):
        wanted = jnp.where(kind == each, offsets(each, wave), wanted)
    wanted = coarse * 40 + jnp.where(wave < WAVES, wanted, 32)
    pick = jnp.where(along == wanted, 1.0, 0.0).astype(jnp.bfloat16)
    spread = jnp.zeros((shape[0], 128), jnp.float32)
    for _ in range(3):
        piece = own.astype(jnp.bfloat16)
        own = own - piece.astype(jnp.float32)
        spread += jnp.dot(pick, piece, preferred_element_type=jnp.float32)
    alone = jnp.where((slab == 0) & (group == 0), 1.0, 0.0)
    shift_ref[...] = (spread[16 * WAVES :] - spread[:16]) * (alone / N**2)
    columns = [
        spread[16 * wave : 16 * (wave + 1)] * ((2.0 - alone) / N**2 if wave == 0 else 2.0 / N**2)
        for wave in range(WAVES)
    ]
    quarter = lax.broadcasted_iota(jnp.int32, (16, 128), 1) // SLABS
    for fine in range(4):
        for half in range(2):
            weight = jnp.zeros((16, 128), jnp.float32)
            for place in range(4):
                weight = jnp.where(quarter == place, turned(columns[4 * half + place], place - fine), weight)
            weight_ref[fine, :, 128 * half : 128 * (half + 1)] = weight


def spectrum_weights(spectrum, nyquist):
    return pl.pallas_call(
        weight_kernel,
        in_specs=[pl.BlockSpec(memory_space=pltpu.VMEM)] * 2,
        out_specs=[pl.BlockSpec(memory_space=pltpu.VMEM)] * 2,
        out_shape=[
            jax.ShapeDtypeStruct((4, 16, LANES), jnp.float32),
            jax.ShapeDtypeStruct((16, 128), jnp.float32),
        ],
        compiler_params=pltpu.CompilerParams(vmem_limit_bytes=16 * 2**20),
        cost_estimate=pl.CostEstimate(flops=10**9, bytes_accessed=2**20, transcendentals=0),
    )(spectrum, nyquist)


def cross_kernel(x_ref, outer_ref, twist_ref, inner_ref, weight_ref, shift_ref, out_ref, za_ref, zb_ref, ze_ref, a_ref, b_ref):
    wide = jnp.float32
    cos, sin = (jnp.concatenate([twist_ref[k], twist_ref[k]], axis=1) for k in range(2))

    def twisted(real, imag):
        return (real * cos + imag * sin).astype(jnp.bfloat16), (imag * cos - real * sin).astype(jnp.bfloat16)

    along = lax.broadcasted_iota(jnp.int32, (2 * SLABS, SLABS * 16), 1) % 16
    extra = jnp.where(along == WAVES, outer_ref[: 2 * SLABS], 0.0).astype(jnp.bfloat16)

    for group in range(GROUPS):
        cells = x_ref[:, group].reshape(SLABS * 16, 2 * LANES)
        mixed = jnp.dot(outer_ref[...], cells, preferred_element_type=wide)
        for wave in range(WAVES):
            rows = pl.ds(SLABS * wave, SLABS)
            for place, ref in enumerate((za_ref, zb_ref)):
                lanes = slice(place * LANES, (place + 1) * LANES)
                first = 2 * SLABS * wave
                real, imag = mixed[first : first + SLABS, lanes], mixed[first + SLABS : first + 2 * SLABS, lanes]
                ref[group, rows, :LANES], ref[group, rows, LANES:] = twisted(real, imag)
        mixed = jnp.dot(extra, cells[:, :LANES], preferred_element_type=wide)
        rows = pl.ds(SLABS * group, SLABS)
        ze_ref[rows, :LANES], ze_ref[rows, LANES:] = twisted(mixed[:SLABS], mixed[SLABS:])

    quarter = lax.broadcasted_iota(jnp.int32, (16, 128), 1) // SLABS
    changes = [jnp.where(quarter == 0, turned(shift_ref[...], -fine), 0.0) for fine in range(4)]
    changes = [jnp.concatenate([change] * ROWS, axis=0) for change in changes]
    weights = [jnp.concatenate([weight_ref[fine]] * ROWS, axis=0) for fine in range(4)]
    below = lax.broadcasted_iota(jnp.int32, (2 * LANES, 128), 0) // 16 % ROWS
    along = lax.broadcasted_iota(jnp.int32, (2 * LANES, 128), 1) // CELLS
    inner = jnp.concatenate(
        [
            jnp.where(below == along + 2 * pair, inner_ref[:, 128 * part : 128 * (part + 1)], 0.0).astype(jnp.bfloat16)
            for part in range(2)
            for pair in range(2)
        ],
        axis=1,
    )
    apart = lax.dot_general(inner, ze_ref[...], NT, preferred_element_type=wide)
    for group in range(GROUPS):
        own = pl.ds(64 * group, 64)
        value = lax.dot_general(inner, za_ref[group], NT, preferred_element_type=wide)
        moved = turned(apart, -group)
        for part in range(2):
            for fine in range(4):
                rows = slice(LANES * part + 64 * fine, LANES * part + 64 * (fine + 1))
                scaled = value[rows] * weights[fine]
                a_ref[part, fine, own, :128] = (scaled[:, :128] + moved[rows] * changes[fine]).astype(jnp.bfloat16)
                a_ref[part, fine, own, 128:] = scaled[:, 128:].astype(jnp.bfloat16)
        value = lax.dot_general(inner, zb_ref[group], NT, preferred_element_type=wide)
        for part in range(2):
            for fine in range(4):
                rows = slice(LANES * part + 64 * fine, LANES * part + 64 * (fine + 1))
                b_ref[part, fine, own] = value[rows].astype(jnp.bfloat16)

    product = jnp.zeros((LANES, LANES), wide)
    for part in range(2):
        for fine in range(4):
            product += lax.dot_general(a_ref[part, fine], b_ref[part, fine], NT, preferred_element_type=wide)
    below = lax.broadcasted_iota(jnp.int32, (LANES, LANES), 0)
    along = lax.broadcasted_iota(jnp.int32, (LANES, LANES), 1)
    product = jnp.where(below % 16 == along % 16, product, 0.0)
    rows = [product[16 * k : 16 * (k + 1)].sum(0, keepdims=True) for k in range(16)]
    rows = jnp.concatenate(rows, axis=0)
    lane = lax.broadcasted_iota(jnp.int32, (16, 128), 1) % 16
    below = lax.broadcasted_iota(jnp.int32, (16, 128), 0) % ROWS
    total = jnp.zeros((16, 128), wide)
    for half in range(2):
        value = rows[:, 128 * half : 128 * (half + 1)]
        for shift in (8, 4, 2, 1):
            near, far = pltpu.roll(value, 128 - shift, 1), pltpu.roll(value, 16 - shift, 1)
            value = value + jnp.where(lane < 16 - shift, near, far)
        total += jnp.where(lane == ROWS * half + below, value, 0.0)
    sums = [total[ROWS * group : ROWS * (group + 1)].sum(0, keepdims=True) for group in range(GROUPS)]
    for slab in range(SLABS):
        for group in range(GROUPS):
            out_ref[slab * GROUPS + group] = sums[group]


def cross_partial(arrived, outer, twist, inner, weight, shift):
    return pl.pallas_call(
        cross_kernel,
        in_specs=[pl.BlockSpec(memory_space=pltpu.VMEM)] * 6,
        out_specs=pl.BlockSpec(memory_space=pltpu.VMEM),
        out_shape=jax.ShapeDtypeStruct((SLABS * GROUPS, 1, 128), jnp.float32),
        scratch_shapes=[
            pltpu.VMEM((GROUPS, LANES, 2 * LANES), jnp.bfloat16),
            pltpu.VMEM((GROUPS, LANES, 2 * LANES), jnp.bfloat16),
            pltpu.VMEM((128, 2 * LANES), jnp.bfloat16),
            pltpu.VMEM((2, 4, LANES, LANES), jnp.bfloat16),
            pltpu.VMEM((2, 4, LANES, LANES), jnp.bfloat16),
        ],
        compiler_params=pltpu.CompilerParams(vmem_limit_bytes=36 * 2**20),
        cost_estimate=pl.CostEstimate(flops=3 * 10**9, bytes_accessed=5 * 2**20, transcendentals=0),
    )(arrived, outer, twist, inner, weight, shift)


def lookup(indices, table):
    onehot = indices[:, None] == jnp.arange(table.shape[0], dtype=jnp.int32)[None, :]
    return jnp.sum(jnp.where(onehot, table[None, :], 0.0), axis=1)


def shards(first_block, second_block, spectrum, first_ids, second_ids, error_scale):
    half, outer, twist, inner = (jnp.asarray(t) for t in make_tables())
    sent = half_transform(first_block.reshape(LANES, N), second_block.reshape(LANES, N), half)
    sent = sent.reshape(SLABS * GROUPS, 16, 2 * LANES)
    arrived = lax.all_to_all(sent, EVERY, 0, 0, tiled=True)
    nyquist = lax.ppermute(spectrum[:1], "grid", [(SLABS // 2, 0)])
    weight, shift = spectrum_weights(spectrum, nyquist)
    arrived = arrived.reshape(SLABS, GROUPS, 16, 2 * LANES)
    partial = cross_partial(arrived, outer, twist, inner, weight, shift)
    partial = lax.all_to_all(partial, EVERY, 0, 0, tiled=True)
    cross = partial.sum((0, 1)).reshape(2, ROWS, 2, 2, ROWS)[:, :, 0]
    cross = cross.transpose(3, 2, 0, 1).reshape(ROWS, GROUPS * ROWS)
    scale_first = lookup(first_ids, error_scale)
    scale_second = lookup(second_ids, error_scale)
    return cross / (N * scale_first[:, None] * scale_second[None, :])


def solution(mesh):
    return jax.shard_map(
        shards,
        mesh=mesh,
        in_specs=(
            P("row", "grid", None),
            P("row", "grid", None),
            P("grid", None),
            P("row"),
            P(),
            P(),
        ),
        out_specs=P("row", None),
        check_vma=False,
    )
```

time: 937 us -> 67.5 us (0.07); the launches traced: 924 us -> 67.2 us
  matrix products: 784 us -> 0 us
  blocking collectives: 62.5 us -> 0 us
  waiting for transfers between devices: 9.29 us -> 39.2 us
  local copies, waits for them, and re-layouts: 22.5 us -> 0.37 us
  between operations: 14.1 us -> 0.16 us
  starting transfers between devices: 29.6 us -> 15.9 us
  Pallas kernels: 0 us -> 10.4 us
    dot_general x15 -> x0, matrix products: 784 us -> none  [the longest x1 66.1 us: shards(): jnp.dot(sine, back_imag, preferred_element_type=wide)]
    psum x1 -> x0, blocking collectives: 62.5 us -> none  [shards(): cross_block = lax.psum(partial_value, 'grid')]
    all_to_all x4 -> x2, waiting for transfers between devices: 9.05 us -> 39.2 us  [the longest x1 29.4 us: shards(): arrived = lax.all_to_all(sent, EVERY, 0, 0, tiled=True)]
    all_to_all x6 -> x0, local copies, waits for them, and re-layouts: 15 us -> none  [the longest x2 5.88 us: shards(): lax.all_to_all(imag_part, 'grid', split_axis=0, concat_axis=1, tiled=True)]
    all_to_all x4 -> x2, starting transfers between devices: 29.1 us -> 15.1 us  [the longest x1 11.5 us: shards(): arrived = lax.all_to_all(sent, EVERY, 0, 0, tiled=True)]
    pallas_call x0 -> x3, Pallas kernels: none -> 10.4 us  [the longest x1 5.43 us: half_transform(): pl.pallas_call(half_kernel, in_specs=[pl.BlockSpec(memory_space=pl.ANY)]...]
  transfers between devices with their start and end apart: 5 -> 3, of which waited for: 1 -> 2; matrix products, arithmetic and copies ran while one was open for 79% -> 1% of each run, Pallas kernels for 0% -> 1%
where the time goes in v1:
time: 67.5 us; the launch traced here: 67.2 us
  waiting for transfers between devices  39.2 us (58%)
  starting transfers between devices  15.9 us (24%)
  Pallas kernels  10.4 us (15%)
  other arithmetic  1.21 us (2%)
    all_to_all x1, waiting for transfers between devices, shards(): arrived = lax.all_to_all(sent, EVERY, 0, 0, tiled=True)  29.4 us
    all_to_all x1, starting transfers between devices, shards(): arrived = lax.all_to_all(sent, EVERY, 0, 0, tiled=True)  11.5 us
    all_to_all x1, waiting for transfers between devices, shards(): partial = lax.all_to_all(partial, EVERY, 0, 0, tiled=True)  9.8 us
    pallas_call x1, Pallas kernels, half_transform(): pl.pallas_call(half_kernel, in_specs=[pl.BlockSpec(memory_space=pl.ANY)]...  5.43 us
    pallas_call x1, Pallas kernels, cross_partial(): pl.pallas_call(cross_kernel, in_specs=[pl.BlockSpec(memory_space=pltpu.VM...  4.52 us
    all_to_all x1, starting transfers between devices, shards(): partial = lax.all_to_all(partial, EVERY, 0, 0, tiled=True)  3.57 us
  transfers between devices with their start and end apart: 3, of which 2 were waited for; matrix products, arithmetic and copies ran while one was open for 1% of the time, Pallas kernels for 1%

profile of v1, /device:TPU:1, one launch (start us, length us, event | category | flops | bytes accessed | tf_op | source)
XLA Modules:
  0.0 67.2 jit_solution(15605564717610018176)
XLA Ops:
  0.0 5.4 %shard_map.100 = bf16[32,4,16,512]{3,2,1,0:T(8,128)(2,1)} custom-call(bf16[256,2048]{1,0:T(8,128)(2,1)} %bitcast.10, bf16[256,2048]{1,0:T(8,128)(2,1)} %bitcast.11, bf16[2048,512]{1,0:T(8,128)(2,1)} %constant.12.clone.table_hbm), custom_call_target="tpu_custom_call" | custom-call | flops 1073741824 | bytes 6291456 | tf_op jit(solution)/shard_map/pallas_call | solution.py:129
  5.4 0.0 copy-start
  5.4 0.0 copy-start.4
  5.5 0.0 copy-start.5
  5.5 11.5 %all-to-all-start = ((bf16[128,16,512]{2,1,0:T(8,128)(2,1)}), bf16[128,16,512]{2,1,0:T(8,128)(2,1)S(1)}, u32[]{:S(2)}, u32[]{:S(2)}) async-start(bf16[128,16,512]{2,1,0:T(8,128)(2,1)} %bitcast.9), calls=%async_computation | async-start | bytes 4194304 | tf_op jit(solution)/shard_map/all_to_all | solution.py:307
  17.0 0.0 copy-done
  17.0 0.0 copy-start.1
  17.0 0.0 copy-start.2
  17.0 0.0 copy-start.3
  17.0 0.8 %collective-permute-start = (f32[1,2048]{1,0:T(1,128)S(1)}, f32[1,2048]{1,0:T(1,128)S(1)}, u32[]{:S(2)}, u32[]{:S(2)}) collective-permute-start(f32[1,2048]{1,0:T(1,128)S(1)} %slice.6), channel_id=1, source_target_pairs={{64,0},{65,1},{66,2},{67,3}} | collective-permute-start | bytes 24584 | tf_op jit(solution)/shard_map/ppermute | solution.py:308
  17.9 0.2 select_reduce_fusion.1
  18.1 0.0 collective-permute-done.nyquist_ref
  18.1 0.5 shard_map.101
  18.6 29.4 %all-to-all-done = bf16[128,16,512]{2,1,0:T(8,128)(2,1)S(1)} async-done(((bf16[128,16,512]{2,1,0:T(8,128)(2,1)}), bf16[128,16,512]{2,1,0:T(8,128)(2,1)S(1)}, u32[]{:S(2)}, u32[]{:S(2)}) %all-to-all-start) | async-done | bytes 2097184 | tf_op jit(solution)/shard_map/all_to_all | solution.py:307
  48.0 0.0 copy-start.6
  48.0 4.5 %shard_map.102 = f32[128,1,128]{2,1,0:T(1,128)} custom-call(bf16[32,4,16,512]{3,2,1,0:T(8,128)(2,1)S(1)} %bitcast.8, bf16[512,512]{1,0:T(8,128)(2,1)S(1)} %copy-done.1, f32[2,32,128]{2,1,0:T(8,128)S(1)} %copy-done.3, bf16[512,256]{1,0:T(8,128)(2,1)S(1)} %copy-done.2, f32[4,16,256]{2,1,0:T(8,128)S(1)} %get-tuple-element.7.weight_ref, ...), custom_call_target="tpu_custom_call" | custom-call | flops 3000000000 | bytes 5242880 | tf_op jit(solution)/shard_map/pallas_call | solution.py:281
  52.5 3.6 %all-to-all-start.1 = ((f32[128,1,128]{2,1,0:T(1,128)}), f32[128,1,128]{2,1,0:T(1,128)S(1)}, u32[]{:S(2)}, u32[]{:S(2)}) async-start(f32[128,1,128]{2,1,0:T(1,128)} %shard_map.102), calls=%async_computation.1 | async-start | bytes 131072 | tf_op jit(solution)/shard_map/all_to_all | solution.py:312
  56.1 0.2 select_reduce_fusion
  56.3 9.8 %all-to-all-done.1 = f32[128,1,128]{2,1,0:T(1,128)S(1)} async-done(((f32[128,1,128]{2,1,0:T(1,128)}), f32[128,1,128]{2,1,0:T(1,128)S(1)}, u32[]{:S(2)}, u32[]{:S(2)}) %all-to-all-start.1) | async-done | bytes 65568 | tf_op jit(solution)/shard_map/all_to_all | solution.py:312
  66.1 0.2 reduce_sum.27
  66.3 0.1 reshape.30
  66.4 0.1 copy.12
  66.5 0.1 reshape.31
  66.6 0.7 multiply_divide_fusion
  (9 shorter events, 0.0 us)
Async XLA Ops:
  5.4 11.5 %copy-start = (f32[64,2048]{1,0:T(8,128)S(1)}, f32[64,2048]{1,0:T(8,128)}, u32[]{:S(2)}) copy-start(f32[64,2048]{1,0:T(8,128)} %spectrum_ref.1) | copy-start | bytes 1572868
  5.4 12.4 %copy-start.4 = (f32[2048]{0:T(1024)S(1)}, f32[2048]{0:T(1024)}, u32[]{:S(2)}) copy-start(f32[2048]{0:T(1024)} %param.15) | copy-start | bytes 24580
  5.5 12.4 %copy-start.5 = (s32[4]{0:T(128)S(1)}, s32[4]{0:T(128)}, u32[]{:S(2)}) copy-start(s32[4]{0:T(128)} %param.13) | copy-start | bytes 52
  5.5 42.5 %all-to-all-start = ((bf16[128,16,512]{2,1,0:T(8,128)(2,1)}), bf16[128,16,512]{2,1,0:T(8,128)(2,1)S(1)}, u32[]{:S(2)}, u32[]{:S(2)}) async-start(bf16[128,16,512]{2,1,0:T(8,128)(2,1)} %bitcast.9), calls=%async_computation | async-start | bytes 4194304 | tf_op jit(solution)/shard_map/all_to_all | solution.py:307
  17.0 31.0 %copy-start.1 = (bf16[512,512]{1,0:T(8,128)(2,1)S(1)}, bf16[512,512]{1,0:T(8,128)(2,1)}, u32[]{:S(2)}) copy-start(bf16[512,512]{1,0:T(8,128)(2,1)} %constant.13.clone.outer_ref) | copy-start | bytes 1572868
  17.0 31.0 %copy-start.2 = (bf16[512,256]{1,0:T(8,128)(2,1)S(1)}, bf16[512,256]{1,0:T(8,128)(2,1)}, u32[]{:S(2)}) copy-start(bf16[512,256]{1,0:T(8,128)(2,1)} %constant.15.clone.inner_ref) | copy-start | bytes 786436
  17.0 31.0 %copy-start.3 = (f32[2,32,128]{2,1,0:T(8,128)S(1)}, f32[2,32,128]{2,1,0:T(8,128)}, u32[]{:S(2)}) copy-start(f32[2,32,128]{2,1,0:T(8,128)} %constant.14.clone.twist_ref) | copy-start | bytes 98308
  17.0 1.0 %collective-permute-start = (f32[1,2048]{1,0:T(1,128)S(1)}, f32[1,2048]{1,0:T(1,128)S(1)}, u32[]{:S(2)}, u32[]{:S(2)}) collective-permute-start(f32[1,2048]{1,0:T(1,128)S(1)} %slice.6), channel_id=1, source_target_pairs={{64,0},{65,1},{66,2},{67,3}} | collective-permute-start | bytes 24584 | tf_op jit(solution)/shard_map/ppermute | solution.py:308
  48.0 8.1 %copy-start.6 = (s32[16]{0:T(128)S(1)}, s32[16]{0:T(128)}, u32[]{:S(2)}) copy-start(s32[16]{0:T(128)} %param.14) | copy-start | bytes 196
  52.5 13.6 %all-to-all-start.1 = ((f32[128,1,128]{2,1,0:T(1,128)}), f32[128,1,128]{2,1,0:T(1,128)S(1)}, u32[]{:S(2)}, u32[]{:S(2)}) async-start(f32[128,1,128]{2,1,0:T(1,128)} %shard_map.102), calls=%async_computation.1 | async-start | bytes 131072 | tf_op jit(solution)/shard_map/all_to_all | solution.py:312

commit v2 on v1

v2 whole, which is shorter than its diff:
```python
import functools
import math

import jax
import jax.numpy as jnp
import ml_dtypes
import numpy as np
from jax import lax
from jax.experimental import pallas as pl
from jax.experimental.pallas import tpu as pltpu
from jax.sharding import PartitionSpec as P

N = 2048
SLABS = 32
GROUPS = 4
CELLS = N // SLABS
ROWS = 4
WAVES = 8
KINDS = 8
LANES = ROWS * CELLS
EVERY = ("grid", "row")

NT = (((1,), (1,)), ((), ()))


def rounded(array):
    return np.asarray(array, np.float64).astype(ml_dtypes.bfloat16)


BASES = (0, 4, 2, 10, 1, 9, 5, 13)


def offsets(kind, j):
    if kind < 2:
        return 8 * j + BASES[kind]
    return 16 * (j // 2) + BASES[kind] + (16 - 2 * BASES[kind]) * (j % 2)


@functools.lru_cache(None)
def make_tables():
    y = np.arange(N // 8)
    j = np.arange(WAVES)
    half = np.zeros((KINDS, SLABS // 2, 2, WAVES, N // 8))
    for kind in range(KINDS):
        for slab in range(SLABS // 2):
            waves = CELLS * (slab + SLABS // 2 * (kind // 4)) + offsets(kind, j)
            if kind < 2:
                angle = 2 * np.pi * ((waves[:, None] * y[None, :]) % N) / N
                half[kind, slab, 0] = np.cos(angle)
                half[kind, slab, 1] = -np.sin(angle)
                continue
            mirror = waves % 16 != BASES[kind]
            waves = np.where(mirror, N - waves, waves)
            angle = 2 * np.pi * ((waves[:, None] * y[None, : N // 16]) % N) / N
            sign = np.where(mirror, -1, 1)[:, None]
            half[kind, slab, 0] = np.concatenate([np.cos(angle), np.sin(angle)], 1)
            half[kind, slab, 1] = sign * np.concatenate([-np.sin(angle), np.cos(angle)], 1)
    half[0, 0, 1, 0] = (-1.0) ** y
    half = rounded(half.reshape(N, N // 8))
    q = np.arange(SLABS).reshape(SLABS // 2, 2).T.reshape(SLABS)
    angle = 2 * np.pi * ((q[:, None] * np.arange(SLABS // 2)[None, :]) % SLABS) / SLABS
    cos, sin = np.cos(angle).reshape(2, SLABS // 2, -1), np.sin(angle).reshape(2, SLABS // 2, -1)
    outer = np.zeros((2, WAVES, 2, SLABS // 2, SLABS // 2, 2, WAVES))
    for k in range(WAVES):
        outer[:, k, 0, :, :, 0, k] = cos
        outer[:, k, 0, :, :, 1, k] = sin
        outer[:, k, 1, :, :, 1, k] = cos
        outer[:, k, 1, :, :, 0, k] = -sin
    outer = rounded(outer.reshape(2, LANES, LANES))
    x = np.arange(CELLS)
    angle = 2 * np.pi * (q[:, None] * x[None, :]) / N
    twist = np.stack([np.tile(np.cos(angle), (1, 2)), np.tile(np.sin(angle), (1, 2))]).astype(np.float32)
    angle = 2 * np.pi * ((x[:, None] * x[None, :]) % CELLS) / CELLS
    cos, sin = np.cos(angle), np.sin(angle)
    inner = np.stack([np.stack([cos, sin], 1), np.stack([-sin, cos], 1)])
    inner = inner.reshape(2, CELLS // 4, 4, 1, 2, 1, CELLS).transpose(0, 2, 3, 1, 4, 5, 6)
    inner = np.broadcast_to(inner, (2, 4, ROWS, CELLS // 4, 2, 2, CELLS))
    inner = rounded(inner.reshape(2 * LANES, LANES))
    return half, outer, twist, inner


SPLIT = 4


def fold(parts):
    even = [parts[k] + parts[k + 8] for k in range(8)]
    odd = [parts[k] - parts[k + 8] for k in range(8)]
    both = [even[k] + even[k + 4] for k in range(4)]
    less = [even[k] - even[k + 4] for k in range(4)]
    yield both[0] + both[2], both[1] + both[3]
    yield both[0] - both[2], both[1] - both[3]
    half = math.sqrt(0.5)
    pairs = [((less[0], -less[2]), (less[1], -less[3]), math.pi / 4)]
    near = [(odd[k], -odd[k + 4]) for k in range(2)]
    far = [(half * (odd[k + 2] - odd[k + 6]), -half * (odd[k + 2] + odd[k + 6])) for k in range(2)]
    pairs.append(tuple((near[k][0] + far[k][0], near[k][1] + far[k][1]) for k in range(2)) + (math.pi / 8,))
    pairs.append(tuple((near[k][0] - far[k][0], near[k][1] - far[k][1]) for k in range(2)) + (5 * math.pi / 8,))
    for (real, imag), (next_real, next_imag), angle in pairs:
        cos, sin = math.cos(angle), math.sin(angle)
        turn_real, turn_imag = cos * next_real + sin * next_imag, cos * next_imag - sin * next_real
        yield real + turn_real, imag + turn_imag
        yield real - turn_real, imag - turn_imag


def half_kernel(a_hbm, b_hbm, table_hbm, out_hbm, block_ref, table_ref, fold_ref, out_ref, block_sem, table_sem, out_sem):
    rows = LANES // SPLIT
    blocks = [
        [
            pltpu.make_async_copy(
                hbm.at[pl.ds(rows * k, rows)], block_ref.at[place, pl.ds(rows * k, rows)], block_sem.at[place, k]
            )
            for k in range(SPLIT)
        ]
        for place, hbm in enumerate((a_hbm, b_hbm))
    ]
    tables = [
        pltpu.make_async_copy(
            table_hbm.at[pl.ds(N // 2 * k, N // 2)], table_ref.at[pl.ds(N // 2 * k, N // 2)], table_sem.at[k]
        )
        for k in range(2)
    ]
    for copy in blocks[0] + tables[:1] + blocks[1] + tables[1:]:
        copy.start()

    for place in range(2):
        for k in range(SPLIT):
            blocks[place][k].wait()

            def fold_rows(step, carry):
                row = pl.multiple_of(rows * k + 16 * step, 16)
                parts = [block_ref[place, pl.ds(row, 16), pl.ds(128 * p, 128)].astype(jnp.float32) for p in range(16)]
                own = pl.ds(pl.multiple_of(LANES * place + row, 16), 16)
                for kind, (first, second) in enumerate(fold(parts)):
                    fold_ref[kind, own, :128] = first.astype(jnp.bfloat16)
                    fold_ref[kind, own, 128:] = second.astype(jnp.bfloat16)
                return carry

            lax.fori_loop(0, rows // 16, fold_rows, 0, unroll=True)
    sends = []
    for kind in range(KINDS):
        if kind % 4 == 0:
            tables[kind // 4].wait()
        value = lax.dot_general(
            table_ref[pl.ds(LANES * kind, LANES), :], fold_ref[kind], NT, preferred_element_type=jnp.float32
        )
        out_ref[kind] = value.astype(jnp.bfloat16).reshape(SLABS // 2, 16, 2 * LANES)
        send = pltpu.make_async_copy(
            out_ref.at[kind], out_hbm.at[pl.ds(SLABS // 2 * (kind // 4), SLABS // 2), kind % 4], out_sem.at[kind]
        )
        send.start()
        sends.append(send)
    for send in sends:
        send.wait()


def half_transform(first, second, table):
    return pl.pallas_call(
        half_kernel,
        in_specs=[pl.BlockSpec(memory_space=pl.ANY)] * 3,
        out_specs=pl.BlockSpec(memory_space=pl.ANY),
        out_shape=jax.ShapeDtypeStruct((SLABS, GROUPS, 16, 2 * LANES), jnp.bfloat16),
        scratch_shapes=[
            pltpu.VMEM((2, LANES, N), jnp.bfloat16),
            pltpu.VMEM((N, N // 8), jnp.bfloat16),
            pltpu.VMEM((KINDS, 2 * LANES, N // 8), jnp.bfloat16),
            pltpu.VMEM((KINDS, SLABS // 2, 16, 2 * LANES), jnp.bfloat16),
            pltpu.SemaphoreType.DMA((2, SPLIT)),
            pltpu.SemaphoreType.DMA((2,)),
            pltpu.SemaphoreType.DMA((KINDS,)),
        ],
        compiler_params=pltpu.CompilerParams(vmem_limit_bytes=60 * 2**20),
        cost_estimate=pl.CostEstimate(flops=N * 512 * 512, bytes_accessed=5 * 2**20, transcendentals=0),
    )(first, second, table)


def turned(value, amount):
    amount = (SLABS * amount) % 128
    return pltpu.roll(value, amount, 1) if amount else value


def weight_kernel(spectrum_ref, nyquist_ref, weight_ref, shift_ref):
    slab, group = lax.axis_index("grid"), lax.axis_index("row")
    own = jnp.concatenate([spectrum_ref[...], jnp.broadcast_to(nyquist_ref[...], (8, N))], axis=0)
    own = jnp.concatenate([own[:, 128 * c : 128 * (c + 1)] for c in range(16)], axis=0)
    mine = 4 * (slab // (SLABS // 2)) + group
    height = CELLS + 8
    shape = ((WAVES + 1) * 16, 16 * height)
    below, along = lax.broadcasted_iota(jnp.int32, (shape[0], 1), 0), lax.broadcasted_iota(jnp.int32, shape, 1)
    wave, coarse = below // 16, below % 16
    wanted = jnp.zeros_like(wave)
    for kind in range(KINDS):
        wanted = jnp.where(mine == kind, offsets(kind, wave), wanted)
    wanted = coarse * height + jnp.where(wave < WAVES, wanted, CELLS)
    pick = jnp.where(along == wanted, 1.0, 0.0).astype(jnp.bfloat16)
    below, along = (lax.broadcasted_iota(jnp.int32, (128, 128), axis) for axis in range(2))
    moved = along // SLABS * SLABS + 2 * (along % 16) + along % SLABS // 16
    order = jnp.where(below == moved, 1.0, 0.0).astype(jnp.bfloat16)
    spread = jnp.zeros((shape[0], 128), jnp.float32)
    for _ in range(3):
        piece = own.astype(jnp.bfloat16)
        own = own - piece.astype(jnp.float32)
        picked = jnp.dot(pick, piece, preferred_element_type=jnp.float32).astype(jnp.bfloat16)
        spread += jnp.dot(picked, order, preferred_element_type=jnp.float32)
    alone = jnp.where((slab == 0) & (group == 0), 1.0, 0.0)
    shift_ref[...] = (spread[16 * WAVES :] - spread[:16]) * (alone / N**2)
    columns = [
        spread[16 * wave : 16 * (wave + 1)] * ((2.0 - alone) / N**2 if wave == 0 else 2.0 / N**2)
        for wave in range(WAVES)
    ]
    quarter = lax.broadcasted_iota(jnp.int32, (16, 128), 1) // SLABS
    for fine in range(4):
        for half in range(2):
            weight = jnp.zeros((16, 128), jnp.float32)
            for place in range(4):
                weight = jnp.where(quarter == place, turned(columns[4 * half + place], place - fine), weight)
            weight_ref[fine, :, 128 * half : 128 * (half + 1)] = weight


def spectrum_weights(spectrum, nyquist):
    return pl.pallas_call(
        weight_kernel,
        in_specs=[pl.BlockSpec(memory_space=pltpu.VMEM)] * 2,
        out_specs=[pl.BlockSpec(memory_space=pltpu.VMEM)] * 2,
        out_shape=[
            jax.ShapeDtypeStruct((4, 16, LANES), jnp.float32),
            jax.ShapeDtypeStruct((16, 128), jnp.float32),
        ],
        compiler_params=pltpu.CompilerParams(vmem_limit_bytes=16 * 2**20),
        cost_estimate=pl.CostEstimate(flops=10**9, bytes_accessed=2**20, transcendentals=0),
    )(spectrum, nyquist)


def cross_kernel(x_ref, outer_ref, twist_ref, inner_ref, weight_ref, shift_ref, out_ref, za_ref, zb_ref, ze_ref, a_ref, b_ref):
    wide = jnp.float32
    cosines, sines = (jnp.concatenate([twist_ref[k], twist_ref[k]], axis=1) for k in range(2))

    nine = lax.broadcasted_iota(jnp.int32, (SLABS, LANES), 1) % 16 == WAVES
    for group in range(GROUPS):
        low, high = x_ref[: SLABS // 2, group], x_ref[SLABS // 2 :, group]
        for odd, cells in enumerate((low + high, low - high)):
            cells = cells.reshape(LANES, 2 * LANES)
            outer = outer_ref[odd]
            mixed = jnp.dot(outer, cells, preferred_element_type=wide)
            step = SLABS // 2
            cos, sin = cosines[step * odd : step * (odd + 1)], sines[step * odd : step * (odd + 1)]

            def twisted(real, imag):
                return (real * cos + imag * sin).astype(jnp.bfloat16), (imag * cos - real * sin).astype(jnp.bfloat16)

            for wave in range(WAVES):
                rows = pl.ds(SLABS * wave + step * odd, step)
                for place, ref in enumerate((za_ref, zb_ref)):
                    lanes = slice(place * LANES, (place + 1) * LANES)
                    first = 2 * step * wave
                    real, imag = mixed[first : first + step, lanes], mixed[first + step : first + 2 * step, lanes]
                    ref[group, rows, :LANES], ref[group, rows, LANES:] = twisted(real, imag)
            extra = jnp.where(nine, outer[:SLABS], 0.0).astype(jnp.bfloat16)
            mixed = jnp.dot(extra, cells[:, :LANES], preferred_element_type=wide)
            rows = pl.ds(SLABS * group + step * odd, step)
            ze_ref[rows, :LANES], ze_ref[rows, LANES:] = twisted(mixed[:step], mixed[step:])

    quarter = lax.broadcasted_iota(jnp.int32, (16, 128), 1) // SLABS
    changes = [jnp.where(quarter == 0, turned(shift_ref[...], -fine), 0.0) for fine in range(4)]
    changes = [jnp.concatenate([change] * ROWS, axis=0) for change in changes]
    weights = [jnp.concatenate([weight_ref[fine]] * ROWS, axis=0) for fine in range(4)]
    below = lax.broadcasted_iota(jnp.int32, (2 * LANES, 128), 0) // 16 % ROWS
    along = lax.broadcasted_iota(jnp.int32, (2 * LANES, 128), 1) // CELLS
    inner = jnp.concatenate(
        [
            jnp.where(below == along + 2 * pair, inner_ref[:, 128 * part : 128 * (part + 1)], 0.0).astype(jnp.bfloat16)
            for part in range(2)
            for pair in range(2)
        ],
        axis=1,
    )
    apart = lax.dot_general(inner, ze_ref[...], NT, preferred_element_type=wide)
    for group in range(GROUPS):
        own = pl.ds(64 * group, 64)
        value = lax.dot_general(inner, za_ref[group], NT, preferred_element_type=wide)
        moved = turned(apart, -group)
        for part in range(2):
            for fine in range(4):
                rows = slice(LANES * part + 64 * fine, LANES * part + 64 * (fine + 1))
                scaled = value[rows] * weights[fine]
                a_ref[part, fine, own, :128] = (scaled[:, :128] + moved[rows] * changes[fine]).astype(jnp.bfloat16)
                a_ref[part, fine, own, 128:] = scaled[:, 128:].astype(jnp.bfloat16)
        value = lax.dot_general(inner, zb_ref[group], NT, preferred_element_type=wide)
        for part in range(2):
            for fine in range(4):
                rows = slice(LANES * part + 64 * fine, LANES * part + 64 * (fine + 1))
                b_ref[part, fine, own] = value[rows].astype(jnp.bfloat16)

    product = jnp.zeros((LANES, LANES), wide)
    for part in range(2):
        for fine in range(4):
            product += lax.dot_general(a_ref[part, fine], b_ref[part, fine], NT, preferred_element_type=wide)
    below = lax.broadcasted_iota(jnp.int32, (LANES, LANES), 0)
    along = lax.broadcasted_iota(jnp.int32, (LANES, LANES), 1)
    product = jnp.where(below % 16 == along % 16, product, 0.0)
    rows = jnp.concatenate([product[16 * k : 16 * (k + 1)].sum(0, keepdims=True) for k in range(16)], axis=0)
    below, along = (lax.broadcasted_iota(jnp.int32, (LANES, 128), axis) for axis in range(2))
    gather = jnp.where(below // 16 == along % 16, 1.0, 0.0).astype(jnp.bfloat16)
    total = jnp.zeros((16, 128), wide)
    for _ in range(3):
        piece = rows.astype(jnp.bfloat16)
        rows = rows - piece.astype(wide)
        total += jnp.dot(piece, gather, preferred_element_type=wide)
    below, along = (lax.broadcasted_iota(jnp.int32, (16, 128), axis) for axis in range(2))
    total = jnp.where(below % ROWS == along // 16, total, 0.0)
    sums = [total[ROWS * group : ROWS * (group + 1)].sum(0, keepdims=True) for group in range(GROUPS)]
    for slab in range(SLABS):
        for group in range(GROUPS):
            out_ref[slab * GROUPS + group] = sums[group]


def cross_partial(arrived, outer, twist, inner, weight, shift):
    return pl.pallas_call(
        cross_kernel,
        in_specs=[pl.BlockSpec(memory_space=pltpu.VMEM)] * 6,
        out_specs=pl.BlockSpec(memory_space=pltpu.VMEM),
        out_shape=jax.ShapeDtypeStruct((SLABS * GROUPS, 1, 128), jnp.float32),
        scratch_shapes=[
            pltpu.VMEM((GROUPS, LANES, 2 * LANES), jnp.bfloat16),
            pltpu.VMEM((GROUPS, LANES, 2 * LANES), jnp.bfloat16),
            pltpu.VMEM((128, 2 * LANES), jnp.bfloat16),
            pltpu.VMEM((2, 4, LANES, LANES), jnp.bfloat16),
            pltpu.VMEM((2, 4, LANES, LANES), jnp.bfloat16),
        ],
        compiler_params=pltpu.CompilerParams(vmem_limit_bytes=36 * 2**20),
        cost_estimate=pl.CostEstimate(flops=3 * 10**9, bytes_accessed=5 * 2**20, transcendentals=0),
    )(arrived, outer, twist, inner, weight, shift)


def lookup(indices, table):
    onehot = indices[:, None] == jnp.arange(table.shape[0], dtype=jnp.int32)[None, :]
    return jnp.sum(jnp.where(onehot, table[None, :], 0.0), axis=1)


def shards(first_block, second_block, spectrum, first_ids, second_ids, error_scale):
    half, outer, twist, inner = (jnp.asarray(t) for t in make_tables())
    sent = half_transform(first_block.reshape(LANES, N), second_block.reshape(LANES, N), half)
    sent = sent.reshape(SLABS * GROUPS, 16, 2 * LANES)
    arrived = lax.all_to_all(sent, EVERY, 0, 0, tiled=True)
    nyquist = lax.ppermute(spectrum[:1], "grid", [(SLABS // 2, 0)])
    weight, shift = spectrum_weights(spectrum, nyquist)
    arrived = arrived.reshape(SLABS, GROUPS, 16, 2 * LANES)
    partial = cross_partial(arrived, outer, twist, inner, weight, shift)
    partial = lax.all_to_all(partial, EVERY, 0, 0, tiled=True)
    cross = partial.sum((0, 1))[:64].reshape(ROWS, GROUPS * ROWS)
    scale_first = lookup(first_ids, error_scale)
    scale_second = lookup(second_ids, error_scale)
    return cross / (N * scale_first[:, None] * scale_second[None, :])


def solution(mesh):
    return jax.shard_map(
        shards,
        mesh=mesh,
        in_specs=(
            P("row", "grid", None),
            P("row", "grid", None),
            P("grid", None),
            P("row"),
            P(),
            P(),
        ),
        out_specs=P("row", None),
        check_vma=False,
    )
```

time: 67.5 us -> 65.1 us (0.964)
  Pallas kernels: 10.4 us -> 8.67 us
    pallas_call x1, Pallas kernels: 5.43 us -> 3.72 us  [half_transform(): pl.pallas_call(half_kernel, in_specs=[pl.BlockSpec(memory_space=pl.ANY)]...]
where the time goes in v2:
time: 65.1 us; the launch traced here: 64.8 us
  waiting for transfers between devices  38.8 us (60%)
  starting transfers between devices  15.9 us (24%)
  Pallas kernels  8.67 us (13%)
  other arithmetic  1.21 us (2%)
    all_to_all x1, waiting for transfers between devices, shards(): arrived = lax.all_to_all(sent, EVERY, 0, 0, tiled=True)  29 us
    all_to_all x1, starting transfers between devices, shards(): arrived = lax.all_to_all(sent, EVERY, 0, 0, tiled=True)  11.5 us
    all_to_all x1, waiting for transfers between devices, shards(): partial = lax.all_to_all(partial, EVERY, 0, 0, tiled=True)  9.8 us
    pallas_call x1, Pallas kernels, cross_partial(): pl.pallas_call(cross_kernel, in_specs=[pl.BlockSpec(memory_space=pltpu.VM...  4.07 us
    pallas_call x1, Pallas kernels, half_transform(): pl.pallas_call(half_kernel, in_specs=[pl.BlockSpec(memory_space=pl.ANY)]...  3.72 us
    all_to_all x1, starting transfers between devices, shards(): partial = lax.all_to_all(partial, EVERY, 0, 0, tiled=True)  3.57 us
  transfers between devices with their start and end apart: 3, of which 2 were waited for; matrix products, arithmetic and copies ran while one was open for 1% of the time, Pallas kernels for 1%

profile of v2, /device:TPU:1, one launch (start us, length us, event | category | flops | bytes accessed | tf_op | source)
XLA Modules:
  0.0 64.8 jit_solution(15265103018913968268)
XLA Ops:
  0.0 3.7 %shard_map.100 = bf16[32,4,16,512]{3,2,1,0:T(8,128)(2,1)} custom-call(bf16[256,2048]{1,0:T(8,128)(2,1)} %bitcast.7, bf16[256,2048]{1,0:T(8,128)(2,1)} %bitcast.8, bf16[2048,256]{1,0:T(8,128)(2,1)} %constant.12.clone.table_hbm), custom_call_target="tpu_custom_call" | custom-call | flops 536870912 | bytes 5242880 | tf_op jit(solution)/shard_map/pallas_call | solution.py:157
  3.7 0.0 copy-start
  3.7 0.0 copy-start.4
  3.8 0.0 copy-start.5
  3.8 11.5 %all-to-all-start = ((bf16[128,16,512]{2,1,0:T(8,128)(2,1)}), bf16[128,16,512]{2,1,0:T(8,128)(2,1)S(1)}, u32[]{:S(2)}, u32[]{:S(2)}) async-start(bf16[128,16,512]{2,1,0:T(8,128)(2,1)} %bitcast.6), calls=%async_computation | async-start | bytes 4194304 | tf_op jit(solution)/shard_map/all_to_all | solution.py:343
  15.3 0.0 copy-done
  15.3 0.0 copy-start.1
  15.3 0.0 copy-start.2
  15.3 0.0 copy-start.3
  15.3 0.8 %collective-permute-start = (f32[1,2048]{1,0:T(1,128)S(1)}, f32[1,2048]{1,0:T(1,128)S(1)}, u32[]{:S(2)}, u32[]{:S(2)}) collective-permute-start(f32[1,2048]{1,0:T(1,128)S(1)} %slice.14), channel_id=1, source_target_pairs={{64,0},{65,1},{66,2},{67,3}} | collective-permute-start | bytes 24584 | tf_op jit(solution)/shard_map/ppermute | solution.py:344
  16.1 0.0 copy-done.4
  16.2 0.2 select_reduce_fusion.1
  16.4 0.0 collective-permute-done.nyquist_ref
  16.4 0.9 %shard_map.101 = (f32[4,16,256]{2,1,0:T(8,128)S(1)}, f32[16,128]{1,0:T(8,128)S(1)}) custom-call(f32[64,2048]{1,0:T(8,128)S(1)} %copy-done, f32[1,2048]{1,0:T(1,128)S(1)} %collective-permute-done.nyquist_ref), custom_call_target="tpu_custom_call" | custom-call | flops 1000000000 | bytes 1048576 | tf_op jit(solution)/shard_map/pallas_call | solution.py:220
  17.3 29.0 %all-to-all-done = bf16[128,16,512]{2,1,0:T(8,128)(2,1)S(1)} async-done(((bf16[128,16,512]{2,1,0:T(8,128)(2,1)}), bf16[128,16,512]{2,1,0:T(8,128)(2,1)S(1)}, u32[]{:S(2)}, u32[]{:S(2)}) %all-to-all-start) | async-done | bytes 2097184 | tf_op jit(solution)/shard_map/all_to_all | solution.py:343
  46.3 0.0 copy-done.3
  46.3 0.0 copy-start.6
  46.3 4.1 %shard_map.102 = f32[128,1,128]{2,1,0:T(1,128)} custom-call(bf16[32,4,16,512]{3,2,1,0:T(8,128)(2,1)S(1)} %bitcast.5, bf16[2,256,256]{2,1,0:T(8,128)(2,1)S(1)} %copy-done.1, f32[2,32,128]{2,1,0:T(8,128)S(1)} %copy-done.3, bf16[512,256]{1,0:T(8,128)(2,1)S(1)} %copy-done.2, f32[4,16,256]{2,1,0:T(8,128)S(1)} %get-tuple-element.7.weight_ref, ...), custom_call_target="tpu_custom_call" | custom-call | flops 3000000000 | bytes 5242880 | tf_op jit(solution)/shard_map/pallas_call | solution.py:317
  50.4 3.6 %all-to-all-start.1 = ((f32[128,1,128]{2,1,0:T(1,128)}), f32[128,1,128]{2,1,0:T(1,128)S(1)}, u32[]{:S(2)}, u32[]{:S(2)}) async-start(f32[128,1,128]{2,1,0:T(1,128)} %shard_map.102), calls=%async_computation.1 | async-start | bytes 131072 | tf_op jit(solution)/shard_map/all_to_all | solution.py:348
  53.9 0.2 select_reduce_fusion
  54.1 9.8 %all-to-all-done.1 = f32[128,1,128]{2,1,0:T(1,128)S(1)} async-done(((f32[128,1,128]{2,1,0:T(1,128)}), f32[128,1,128]{2,1,0:T(1,128)S(1)}, u32[]{:S(2)}, u32[]{:S(2)}) %all-to-all-start.1) | async-done | bytes 65568 | tf_op jit(solution)/shard_map/all_to_all | solution.py:348
  64.0 0.2 reduce_sum.27
  64.1 0.1 reshape.35
  64.2 0.7 %multiply_divide_fusion = f32[4,16]{1,0:T(4,128)} fusion(f32[4,16]{1,0:T(4,128)S(1)} %reshape.35, f32[16]{0:T(128)S(1)} %select_reduce_fusion, f32[4]{0:T(128)S(1)} %broadcast_multiply_fusion), kind=kLoop, calls=%fused_computation.4 | loop fusion | flops 128 | bytes 592 | tf_op jit(solution)/shard_map/div | solution.py:352
  (6 shorter events, 0.0 us)
Async XLA Ops:
  3.7 11.6 %copy-start = (f32[64,2048]{1,0:T(8,128)S(1)}, f32[64,2048]{1,0:T(8,128)}, u32[]{:S(2)}) copy-start(f32[64,2048]{1,0:T(8,128)} %spectrum_ref.1) | copy-start | bytes 1572868
  3.7 12.4 %copy-start.4 = (f32[2048]{0:T(1024)S(1)}, f32[2048]{0:T(1024)}, u32[]{:S(2)}) copy-start(f32[2048]{0:T(1024)} %param.15) | copy-start | bytes 24580
  3.8 12.4 %copy-start.5 = (s32[4]{0:T(128)S(1)}, s32[4]{0:T(128)}, u32[]{:S(2)}) copy-start(s32[4]{0:T(128)} %param.13) | copy-start | bytes 52
  3.8 42.5 %all-to-all-start = ((bf16[128,16,512]{2,1,0:T(8,128)(2,1)}), bf16[128,16,512]{2,1,0:T(8,128)(2,1)S(1)}, u32[]{:S(2)}, u32[]{:S(2)}) async-start(bf16[128,16,512]{2,1,0:T(8,128)(2,1)} %bitcast.6), calls=%async_computation | async-start | bytes 4194304 | tf_op jit(solution)/shard_map/all_to_all | solution.py:343
  15.3 31.0 %copy-start.1 = (bf16[2,256,256]{2,1,0:T(8,128)(2,1)S(1)}, bf16[2,256,256]{2,1,0:T(8,128)(2,1)}, u32[]{:S(2)}) copy-start(bf16[2,256,256]{2,1,0:T(8,128)(2,1)} %constant.13.clone.outer_ref) | copy-start | bytes 786436
  15.3 31.0 %copy-start.2 = (bf16[512,256]{1,0:T(8,128)(2,1)S(1)}, bf16[512,256]{1,0:T(8,128)(2,1)}, u32[]{:S(2)}) copy-start(bf16[512,256]{1,0:T(8,128)(2,1)} %constant.15.clone.inner_ref) | copy-start | bytes 786436
  15.3 31.0 %copy-start.3 = (f32[2,32,128]{2,1,0:T(8,128)S(1)}, f32[2,32,128]{2,1,0:T(8,128)}, u32[]{:S(2)}) copy-start(f32[2,32,128]{2,1,0:T(8,128)} %constant.14.clone.twist_ref) | copy-start | bytes 98308
  15.3 1.0 %collective-permute-start = (f32[1,2048]{1,0:T(1,128)S(1)}, f32[1,2048]{1,0:T(1,128)S(1)}, u32[]{:S(2)}, u32[]{:S(2)}) collective-permute-start(f32[1,2048]{1,0:T(1,128)S(1)} %slice.14), channel_id=1, source_target_pairs={{64,0},{65,1},{66,2},{67,3}} | collective-permute-start | bytes 24584 | tf_op jit(solution)/shard_map/ppermute | solution.py:344
  46.3 7.7 %copy-start.6 = (s32[16]{0:T(128)S(1)}, s32[16]{0:T(128)}, u32[]{:S(2)}) copy-start(s32[16]{0:T(128)} %param.14) | copy-start | bytes 196
  50.4 13.6 %all-to-all-start.1 = ((f32[128,1,128]{2,1,0:T(1,128)}), f32[128,1,128]{2,1,0:T(1,128)S(1)}, u32[]{:S(2)}, u32[]{:S(2)}) async-start(f32[128,1,128]{2,1,0:T(1,128)} %shard_map.102), calls=%async_computation.1 | async-start | bytes 131072 | tf_op jit(solution)/shard_map/all_to_all | solution.py:348

commit v3 on v2

--- a/solution.py
+++ b/solution.py
@@ -71,11 +71,14 @@
     angle = 2 * np.pi * (q[:, None] * x[None, :]) / N
     twist = np.stack([np.tile(np.cos(angle), (1, 2)), np.tile(np.sin(angle), (1, 2))]).astype(np.float32)
     angle = 2 * np.pi * ((x[:, None] * x[None, :]) % CELLS) / CELLS
-    cos, sin = np.cos(angle), np.sin(angle)
-    inner = np.stack([np.stack([cos, sin], 1), np.stack([-sin, cos], 1)])
-    inner = inner.reshape(2, CELLS // 4, 4, 1, 2, 1, CELLS).transpose(0, 2, 3, 1, 4, 5, 6)
-    inner = np.broadcast_to(inner, (2, 4, ROWS, CELLS // 4, 2, 2, CELLS))
-    inner = rounded(inner.reshape(2 * LANES, LANES))
+    cos, sin = (t.reshape(CELLS // 4, 4, CELLS).transpose(1, 0, 2) for t in (np.cos(angle), np.sin(angle)))
+    inner = np.zeros((2, 4, 2, CELLS // 4, 2, 2, CELLS))
+    for k in range(2):
+        inner[0, :, k, :, 0, k] = cos
+        inner[0, :, k, :, 1, k] = sin
+        inner[1, :, k, :, 1, k] = cos
+        inner[1, :, k, :, 0, k] = -sin
+    inner = rounded(inner.reshape(LANES, LANES))
     return half, outer, twist, inner
 
 
@@ -234,61 +237,57 @@
     wide = jnp.float32
     cosines, sines = (jnp.concatenate([twist_ref[k], twist_ref[k]], axis=1) for k in range(2))
 
+    step = SLABS // 2
     nine = lax.broadcasted_iota(jnp.int32, (SLABS, LANES), 1) % 16 == WAVES
+    outers = [
+        jnp.concatenate([outer_ref[odd], jnp.where(nine, outer_ref[odd, :SLABS], 0.0).astype(jnp.bfloat16)], axis=0)
+        for odd in range(2)
+    ]
+
+    def twist(mixed, first, odd, ref, rows):
+        real, imag = mixed[first : first + step], mixed[first + step : first + 2 * step]
+        cos, sin = cosines[step * odd : step * (odd + 1)], sines[step * odd : step * (odd + 1)]
+        new_real = (real * cos + imag * sin).astype(jnp.bfloat16)
+        new_imag = (imag * cos - real * sin).astype(jnp.bfloat16)
+        for pair in range(2):
+            lanes = slice(128 * pair, 128 * (pair + 1))
+            ref[pair, rows, :128], ref[pair, rows, 128:] = new_real[:, lanes], new_imag[:, lanes]
+
     for group in range(GROUPS):
-        low, high = x_ref[: SLABS // 2, group], x_ref[SLABS // 2 :, group]
+        low, high = x_ref[:step, group], x_ref[step:, group]
         for odd, cells in enumerate((low + high, low - high)):
             cells = cells.reshape(LANES, 2 * LANES)
-            outer = outer_ref[odd]
-            mixed = jnp.dot(outer, cells, preferred_element_type=wide)
-            step = SLABS // 2
-            cos, sin = cosines[step * odd : step * (odd + 1)], sines[step * odd : step * (odd + 1)]
-
-            def twisted(real, imag):
-                return (real * cos + imag * sin).astype(jnp.bfloat16), (imag * cos - real * sin).astype(jnp.bfloat16)
-
+            left = jnp.dot(outers[odd], cells[:, :LANES], preferred_element_type=wide)
+            right = jnp.dot(outer_ref[odd], cells[:, LANES:], preferred_element_type=wide)
             for wave in range(WAVES):
                 rows = pl.ds(SLABS * wave + step * odd, step)
-                for place, ref in enumerate((za_ref, zb_ref)):
-                    lanes = slice(place * LANES, (place + 1) * LANES)
-                    first = 2 * step * wave
-                    real, imag = mixed[first : first + step, lanes], mixed[first + step : first + 2 * step, lanes]
-                    ref[group, rows, :LANES], ref[group, rows, LANES:] = twisted(real, imag)
-            extra = jnp.where(nine, outer[:SLABS], 0.0).astype(jnp.bfloat16)
-            mixed = jnp.dot(extra, cells[:, :LANES], preferred_element_type=wide)
-            rows = pl.ds(SLABS * group + step * odd, step)
-            ze_ref[rows, :LANES], ze_ref[rows, LANES:] = twisted(mixed[:step], mixed[step:])
+                twist(left, SLABS * wave, odd, za_ref.at[group], rows)
+                twist(right, SLABS * wave, odd, zb_ref.at[group], rows)
+            twist(left, SLABS * WAVES, odd, ze_ref, pl.ds(SLABS * group + step * odd, step))
 
     quarter = lax.broadcasted_iota(jnp.int32, (16, 128), 1) // SLABS
     changes = [jnp.where(quarter == 0, turned(shift_ref[...], -fine), 0.0) for fine in range(4)]
-    changes = [jnp.concatenate([change] * ROWS, axis=0) for change in changes]
-    weights = [jnp.concatenate([weight_ref[fine]] * ROWS, axis=0) for fine in range(4)]
-    below = lax.broadcasted_iota(jnp.int32, (2 * LANES, 128), 0) // 16 % ROWS
-    along = lax.broadcasted_iota(jnp.int32, (2 * LANES, 128), 1) // CELLS
-    inner = jnp.concatenate(
-        [
-            jnp.where(below == along + 2 * pair, inner_ref[:, 128 * part : 128 * (part + 1)], 0.0).astype(jnp.bfloat16)
-            for part in range(2)
-            for pair in range(2)
-        ],
-        axis=1,
-    )
-    apart = lax.dot_general(inner, ze_ref[...], NT, preferred_element_type=wide)
-    for group in range(GROUPS):
-        own = pl.ds(64 * group, 64)
-        value = lax.dot_general(inner, za_ref[group], NT, preferred_element_type=wide)
-        moved = turned(apart, -group)
-        for part in range(2):
-            for fine in range(4):
-                rows = slice(LANES * part + 64 * fine, LANES * part + 64 * (fine + 1))
-                scaled = value[rows] * weights[fine]
-                a_ref[part, fine, own, :128] = (scaled[:, :128] + moved[rows] * changes[fine]).astype(jnp.bfloat16)
-                a_ref[part, fine, own, 128:] = scaled[:, 128:].astype(jnp.bfloat16)
-        value = lax.dot_general(inner, zb_ref[group], NT, preferred_element_type=wide)
-        for part in range(2):
-            for fine in range(4):
-                rows = slice(LANES * part + 64 * fine, LANES * part + 64 * (fine + 1))
-                b_ref[part, fine, own] = value[rows].astype(jnp.bfloat16)
+    changes = [jnp.concatenate([change] * 2, axis=0) for change in changes]
+    weights = [jnp.concatenate([weight_ref[fine]] * 2, axis=0) for fine in range(4)]
+    inner = inner_ref[...]
+    for pair in range(2):
+        apart = lax.dot_general(inner, ze_ref[pair], NT, preferred_element_type=wide)
+        for group in range(GROUPS):
+            own = pl.ds(64 * group + 32 * pair, 32)
+            value = lax.dot_general(inner, za_ref[group, pair], NT, preferred_element_type=wide)
+            moved = turned(apart, -group)
+            for part in range(2):
+                for fine in range(4):
+                    rows = slice(128 * part + 32 * fine, 128 * part + 32 * (fine + 1))
+                    scaled = value[rows] * weights[fine]
+                    changed = scaled[:, :128] + moved[rows] * changes[fine]
+                    a_ref[part, fine, own, :128] = changed.astype(jnp.bfloat16)
+                    a_ref[part, fine, own, 128:] = scaled[:, 128:].astype(jnp.bfloat16)
+            value = lax.dot_general(inner, zb_ref[group, pair], NT, preferred_element_type=wide)
+            for part in range(2):
+                for fine in range(4):
+                    rows = slice(128 * part + 32 * fine, 128 * part + 32 * (fine + 1))
+                    b_ref[part, fine, own] = value[rows].astype(jnp.bfloat16)
 
     product = jnp.zeros((LANES, LANES), wide)
     for part in range(2):
@@ -320,9 +319,9 @@
         out_specs=pl.BlockSpec(memory_space=pltpu.VMEM),
         out_shape=jax.ShapeDtypeStruct((SLABS * GROUPS, 1, 128), jnp.float32),
         scratch_shapes=[
-            pltpu.VMEM((GROUPS, LANES, 2 * LANES), jnp.bfloat16),
-            pltpu.VMEM((GROUPS, LANES, 2 * LANES), jnp.bfloat16),
-            pltpu.VMEM((128, 2 * LANES), jnp.bfloat16),
+            pltpu.VMEM((GROUPS, 2, LANES, LANES), jnp.bfloat16),
+            pltpu.VMEM((GROUPS, 2, LANES, LANES), jnp.bfloat16),
+            pltpu.VMEM((2, 128, LANES), jnp.bfloat16),
             pltpu.VMEM((2, 4, LANES, LANES), jnp.bfloat16),
             pltpu.VMEM((2, 4, LANES, LANES), jnp.bfloat16),
         ],

time: 65.1 us -> 64.1 us (0.985)
  Pallas kernels: 8.67 us -> 7.71 us
    pallas_call x1, Pallas kernels: 4.07 us -> 3.1 us  [cross_partial(): pl.pallas_call(cross_kernel, in_specs=[pl.BlockSpec(memory_space=pltpu.VM...]
where the time goes in v3:
time: 64.1 us; the launch traced here: 63.9 us
  waiting for transfers between devices  38.8 us (61%)
  starting transfers between devices  15.9 us (25%)
  Pallas kernels  7.71 us (12%)
  other arithmetic  1.21 us (2%)
    all_to_all x1, waiting for transfers between devices, shards(): arrived = lax.all_to_all(sent, EVERY, 0, 0, tiled=True)  29 us
    all_to_all x1, starting transfers between devices, shards(): arrived = lax.all_to_all(sent, EVERY, 0, 0, tiled=True)  11.5 us
    all_to_all x1, waiting for transfers between devices, shards(): partial = lax.all_to_all(partial, EVERY, 0, 0, tiled=True)  9.8 us
    pallas_call x1, Pallas kernels, half_transform(): pl.pallas_call(half_kernel, in_specs=[pl.BlockSpec(memory_space=pl.ANY)]...  3.72 us
    all_to_all x1, starting transfers between devices, shards(): partial = lax.all_to_all(partial, EVERY, 0, 0, tiled=True)  3.57 us
    pallas_call x1, Pallas kernels, cross_partial(): pl.pallas_call(cross_kernel, in_specs=[pl.BlockSpec(memory_space=pltpu.VM...  3.1 us
  transfers between devices with their start and end apart: 3, of which 2 were waited for; matrix products, arithmetic and copies ran while one was open for 1% of the time, Pallas kernels for 1%

profile of v3, /device:TPU:1, one launch (start us, length us, event | category | flops | bytes accessed | tf_op | source)
XLA Modules:
  0.0 63.9 jit_solution(4660463935383670515)
XLA Ops:
  0.0 3.7 %shard_map.100 = bf16[32,4,16,512]{3,2,1,0:T(8,128)(2,1)} custom-call(bf16[256,2048]{1,0:T(8,128)(2,1)} %bitcast.7, bf16[256,2048]{1,0:T(8,128)(2,1)} %bitcast.8, bf16[2048,256]{1,0:T(8,128)(2,1)} %constant.12.clone.table_hbm), custom_call_target="tpu_custom_call" | custom-call | flops 536870912 | bytes 5242880 | tf_op jit(solution)/shard_map/pallas_call | solution.py:160
  3.7 0.0 copy-start
  3.7 0.0 copy-start.4
  3.8 0.0 copy-start.5
  3.8 11.5 %all-to-all-start = ((bf16[128,16,512]{2,1,0:T(8,128)(2,1)}), bf16[128,16,512]{2,1,0:T(8,128)(2,1)S(1)}, u32[]{:S(2)}, u32[]{:S(2)}) async-start(bf16[128,16,512]{2,1,0:T(8,128)(2,1)} %bitcast.6), calls=%async_computation | async-start | bytes 4194304 | tf_op jit(solution)/shard_map/all_to_all | solution.py:342
  15.3 0.0 copy-done
  15.3 0.0 copy-start.1
  15.3 0.0 copy-start.2
  15.3 0.0 copy-start.3
  15.3 0.8 %collective-permute-start = (f32[1,2048]{1,0:T(1,128)S(1)}, f32[1,2048]{1,0:T(1,128)S(1)}, u32[]{:S(2)}, u32[]{:S(2)}) collective-permute-start(f32[1,2048]{1,0:T(1,128)S(1)} %slice.14), channel_id=1, source_target_pairs={{64,0},{65,1},{66,2},{67,3}} | collective-permute-start | bytes 24584 | tf_op jit(solution)/shard_map/ppermute | solution.py:343
  16.1 0.0 copy-done.4
  16.2 0.2 select_reduce_fusion.1
  16.4 0.0 collective-permute-done.nyquist_ref
  16.4 0.9 %shard_map.101 = (f32[4,16,256]{2,1,0:T(8,128)S(1)}, f32[16,128]{1,0:T(8,128)S(1)}) custom-call(f32[64,2048]{1,0:T(8,128)S(1)} %copy-done, f32[1,2048]{1,0:T(1,128)S(1)} %collective-permute-done.nyquist_ref), custom_call_target="tpu_custom_call" | custom-call | flops 1000000000 | bytes 1048576 | tf_op jit(solution)/shard_map/pallas_call | solution.py:223
  17.3 29.0 %all-to-all-done = bf16[128,16,512]{2,1,0:T(8,128)(2,1)S(1)} async-done(((bf16[128,16,512]{2,1,0:T(8,128)(2,1)}), bf16[128,16,512]{2,1,0:T(8,128)(2,1)S(1)}, u32[]{:S(2)}, u32[]{:S(2)}) %all-to-all-start) | async-done | bytes 2097184 | tf_op jit(solution)/shard_map/all_to_all | solution.py:342
  46.3 0.0 copy-done.3
  46.3 0.0 copy-start.6
  46.3 3.1 %shard_map.102 = f32[128,1,128]{2,1,0:T(1,128)} custom-call(bf16[32,4,16,512]{3,2,1,0:T(8,128)(2,1)S(1)} %bitcast.5, bf16[2,256,256]{2,1,0:T(8,128)(2,1)S(1)} %copy-done.1, f32[2,32,128]{2,1,0:T(8,128)S(1)} %copy-done.3, bf16[256,256]{1,0:T(8,128)(2,1)S(1)} %copy-done.2, f32[4,16,256]{2,1,0:T(8,128)S(1)} %get-tuple-element.7.weight_ref, ...), custom_call_target="tpu_custom_call" | custom-call | flops 3000000000 | bytes 5242880 | tf_op jit(solution)/shard_map/pallas_call | solution.py:316
  49.4 3.6 %all-to-all-start.1 = ((f32[128,1,128]{2,1,0:T(1,128)}), f32[128,1,128]{2,1,0:T(1,128)S(1)}, u32[]{:S(2)}, u32[]{:S(2)}) async-start(f32[128,1,128]{2,1,0:T(1,128)} %shard_map.102), calls=%async_computation.1 | async-start | bytes 131072 | tf_op jit(solution)/shard_map/all_to_all | solution.py:347
  53.0 0.2 select_reduce_fusion
  53.2 9.8 %all-to-all-done.1 = f32[128,1,128]{2,1,0:T(1,128)S(1)} async-done(((f32[128,1,128]{2,1,0:T(1,128)}), f32[128,1,128]{2,1,0:T(1,128)S(1)}, u32[]{:S(2)}, u32[]{:S(2)}) %all-to-all-start.1) | async-done | bytes 65568 | tf_op jit(solution)/shard_map/all_to_all | solution.py:347
  63.0 0.2 reduce_sum.27
  63.1 0.1 reshape.35
  63.2 0.7 %multiply_divide_fusion = f32[4,16]{1,0:T(4,128)} fusion(f32[4,16]{1,0:T(4,128)S(1)} %reshape.35, f32[16]{0:T(128)S(1)} %select_reduce_fusion, f32[4]{0:T(128)S(1)} %broadcast_multiply_fusion), kind=kLoop, calls=%fused_computation.4 | loop fusion | flops 128 | bytes 592 | tf_op jit(solution)/shard_map/div | solution.py:351
  (6 shorter events, 0.0 us)
Async XLA Ops:
  3.7 11.6 %copy-start = (f32[64,2048]{1,0:T(8,128)S(1)}, f32[64,2048]{1,0:T(8,128)}, u32[]{:S(2)}) copy-start(f32[64,2048]{1,0:T(8,128)} %spectrum_ref.1) | copy-start | bytes 1572868
  3.7 12.4 %copy-start.4 = (f32[2048]{0:T(1024)S(1)}, f32[2048]{0:T(1024)}, u32[]{:S(2)}) copy-start(f32[2048]{0:T(1024)} %param.15) | copy-start | bytes 24580
  3.8 12.4 %copy-start.5 = (s32[4]{0:T(128)S(1)}, s32[4]{0:T(128)}, u32[]{:S(2)}) copy-start(s32[4]{0:T(128)} %param.13) | copy-start | bytes 52
  3.8 42.5 %all-to-all-start = ((bf16[128,16,512]{2,1,0:T(8,128)(2,1)}), bf16[128,16,512]{2,1,0:T(8,128)(2,1)S(1)}, u32[]{:S(2)}, u32[]{:S(2)}) async-start(bf16[128,16,512]{2,1,0:T(8,128)(2,1)} %bitcast.6), calls=%async_computation | async-start | bytes 4194304 | tf_op jit(solution)/shard_map/all_to_all | solution.py:342
  15.3 31.0 %copy-start.1 = (bf16[2,256,256]{2,1,0:T(8,128)(2,1)S(1)}, bf16[2,256,256]{2,1,0:T(8,128)(2,1)}, u32[]{:S(2)}) copy-start(bf16[2,256,256]{2,1,0:T(8,128)(2,1)} %constant.13.clone.outer_ref) | copy-start | bytes 786436
  15.3 31.0 %copy-start.2 = (bf16[256,256]{1,0:T(8,128)(2,1)S(1)}, bf16[256,256]{1,0:T(8,128)(2,1)}, u32[]{:S(2)}) copy-start(bf16[256,256]{1,0:T(8,128)(2,1)} %constant.15.clone.inner_ref) | copy-start | bytes 393220
  15.3 31.0 %copy-start.3 = (f32[2,32,128]{2,1,0:T(8,128)S(1)}, f32[2,32,128]{2,1,0:T(8,128)}, u32[]{:S(2)}) copy-start(f32[2,32,128]{2,1,0:T(8,128)} %constant.14.clone.twist_ref) | copy-start | bytes 98308
  15.3 1.0 %collective-permute-start = (f32[1,2048]{1,0:T(1,128)S(1)}, f32[1,2048]{1,0:T(1,128)S(1)}, u32[]{:S(2)}, u32[]{:S(2)}) collective-permute-start(f32[1,2048]{1,0:T(1,128)S(1)} %slice.14), channel_id=1, source_target_pairs={{64,0},{65,1},{66,2},{67,3}} | collective-permute-start | bytes 24584 | tf_op jit(solution)/shard_map/ppermute | solution.py:343
  46.3 6.7 %copy-start.6 = (s32[16]{0:T(128)S(1)}, s32[16]{0:T(128)}, u32[]{:S(2)}) copy-start(s32[16]{0:T(128)} %param.14) | copy-start | bytes 196
  49.4 13.6 %all-to-all-start.1 = ((f32[128,1,128]{2,1,0:T(1,128)}), f32[128,1,128]{2,1,0:T(1,128)S(1)}, u32[]{:S(2)}, u32[]{:S(2)}) async-start(f32[128,1,128]{2,1,0:T(1,128)} %shard_map.102), calls=%async_computation.1 | async-start | bytes 131072 | tf_op jit(solution)/shard_map/all_to_all | solution.py:347

commit v4 on v3

--- a/solution.py
+++ b/solution.py
@@ -18,7 +18,7 @@
 WAVES = 8
 KINDS = 8
 LANES = ROWS * CELLS
-EVERY = ("grid", "row")
+EVERY = ("row", "grid")
 
 NT = (((1,), (1,)), ((), ()))
 
@@ -122,7 +122,7 @@
         )
         for k in range(2)
     ]
-    for copy in blocks[0] + tables[:1] + blocks[1] + tables[1:]:
+    for copy in blocks[0] + blocks[1] + tables:
         copy.start()
 
     for place in range(2):
@@ -148,7 +148,7 @@
         )
         out_ref[kind] = value.astype(jnp.bfloat16).reshape(SLABS // 2, 16, 2 * LANES)
         send = pltpu.make_async_copy(
-            out_ref.at[kind], out_hbm.at[pl.ds(SLABS // 2 * (kind // 4), SLABS // 2), kind % 4], out_sem.at[kind]
+            out_ref.at[kind], out_hbm.at[kind % 4, pl.ds(SLABS // 2 * (kind // 4), SLABS // 2)], out_sem.at[kind]
         )
         send.start()
         sends.append(send)
@@ -161,7 +161,7 @@
         half_kernel,
         in_specs=[pl.BlockSpec(memory_space=pl.ANY)] * 3,
         out_specs=pl.BlockSpec(memory_space=pl.ANY),
-        out_shape=jax.ShapeDtypeStruct((SLABS, GROUPS, 16, 2 * LANES), jnp.bfloat16),
+        out_shape=jax.ShapeDtypeStruct((GROUPS, SLABS, 16, 2 * LANES), jnp.bfloat16),
         scratch_shapes=[
             pltpu.VMEM((2, LANES, N), jnp.bfloat16),
             pltpu.VMEM((N, N // 8), jnp.bfloat16),
@@ -253,8 +253,19 @@
             lanes = slice(128 * pair, 128 * (pair + 1))
             ref[pair, rows, :128], ref[pair, rows, 128:] = new_real[:, lanes], new_imag[:, lanes]
 
+    inner = inner_ref[...]
+
+    def right_cells(group):
+        for pair in range(2):
+            own = pl.ds(64 * group + 32 * pair, 32)
+            value = lax.dot_general(inner, zb_ref[group, pair], NT, preferred_element_type=wide)
+            for part in range(2):
+                for fine in range(4):
+                    rows = slice(128 * part + 32 * fine, 128 * part + 32 * (fine + 1))
+                    b_ref[part, fine, own] = value[rows].astype(jnp.bfloat16)
+
     for group in range(GROUPS):
-        low, high = x_ref[:step, group], x_ref[step:, group]
+        low, high = x_ref[group, :step], x_ref[group, step:]
         for odd, cells in enumerate((low + high, low - high)):
             cells = cells.reshape(LANES, 2 * LANES)
             left = jnp.dot(outers[odd], cells[:, :LANES], preferred_element_type=wide)
@@ -264,12 +275,14 @@
                 twist(left, SLABS * wave, odd, za_ref.at[group], rows)
                 twist(right, SLABS * wave, odd, zb_ref.at[group], rows)
             twist(left, SLABS * WAVES, odd, ze_ref, pl.ds(SLABS * group + step * odd, step))
+        if group:
+            right_cells(group - 1)
+    right_cells(GROUPS - 1)
 
     quarter = lax.broadcasted_iota(jnp.int32, (16, 128), 1) // SLABS
     changes = [jnp.where(quarter == 0, turned(shift_ref[...], -fine), 0.0) for fine in range(4)]
     changes = [jnp.concatenate([change] * 2, axis=0) for change in changes]
     weights = [jnp.concatenate([weight_ref[fine]] * 2, axis=0) for fine in range(4)]
-    inner = inner_ref[...]
     for pair in range(2):
         apart = lax.dot_general(inner, ze_ref[pair], NT, preferred_element_type=wide)
         for group in range(GROUPS):
@@ -283,11 +296,6 @@
                     changed = scaled[:, :128] + moved[rows] * changes[fine]
                     a_ref[part, fine, own, :128] = changed.astype(jnp.bfloat16)
                     a_ref[part, fine, own, 128:] = scaled[:, 128:].astype(jnp.bfloat16)
-            value = lax.dot_general(inner, zb_ref[group, pair], NT, preferred_element_type=wide)
-            for part in range(2):
-                for fine in range(4):
-                    rows = slice(128 * part + 32 * fine, 128 * part + 32 * (fine + 1))
-                    b_ref[part, fine, own] = value[rows].astype(jnp.bfloat16)
 
     product = jnp.zeros((LANES, LANES), wide)
     for part in range(2):
@@ -309,7 +317,7 @@
     sums = [total[ROWS * group : ROWS * (group + 1)].sum(0, keepdims=True) for group in range(GROUPS)]
     for slab in range(SLABS):
         for group in range(GROUPS):
-            out_ref[slab * GROUPS + group] = sums[group]
+            out_ref[group * SLABS + slab] = sums[group]
 
 
 def cross_partial(arrived, outer, twist, inner, weight, shift):
@@ -342,13 +350,12 @@
     arrived = lax.all_to_all(sent, EVERY, 0, 0, tiled=True)
     nyquist = lax.ppermute(spectrum[:1], "grid", [(SLABS // 2, 0)])
     weight, shift = spectrum_weights(spectrum, nyquist)
-    arrived = arrived.reshape(SLABS, GROUPS, 16, 2 * LANES)
+    arrived = arrived.reshape(GROUPS, SLABS, 16, 2 * LANES)
     partial = cross_partial(arrived, outer, twist, inner, weight, shift)
+    factor = 1.0 / (N * lookup(first_ids, error_scale)[:, None] * lookup(second_ids, error_scale)[None, :])
+    partial, factor = lax.optimization_barrier((partial, factor))
     partial = lax.all_to_all(partial, EVERY, 0, 0, tiled=True)
-    cross = partial.sum((0, 1))[:64].reshape(ROWS, GROUPS * ROWS)
-    scale_first = lookup(first_ids, error_scale)
-    scale_second = lookup(second_ids, error_scale)
-    return cross / (N * scale_first[:, None] * scale_second[None, :])
+    return partial.sum((0, 1))[:64].reshape(ROWS, GROUPS * ROWS) * factor
 
 
 def solution(mesh):

time: 64.1 us -> 62.5 us (0.975)
  blocking collectives: 0 us -> 13.6 us
  waiting for transfers between devices: 38.8 us -> 28 us
  starting transfers between devices: 15.9 us -> 12.3 us
  Pallas kernels: 7.71 us -> 6.95 us
    all_to_all x0 -> x1, blocking collectives: none -> 13.6 us  [shards(): partial = lax.all_to_all(partial, EVERY, 0, 0, tiled=True)]
    all_to_all x1 -> x0, waiting for transfers between devices: 9.8 us -> none  [shards(): partial = lax.all_to_all(partial, EVERY, 0, 0, tiled=True)]
    all_to_all x1 -> x0, starting transfers between devices: 3.57 us -> none  [shards(): partial = lax.all_to_all(partial, EVERY, 0, 0, tiled=True)]
    all_to_all x1, waiting for transfers between devices: 29 us -> 28 us  [shards(): arrived = lax.all_to_all(sent, EVERY, 0, 0, tiled=True)]
    pallas_call x1, Pallas kernels: 3.1 us -> 2.37 us  [cross_partial(): pl.pallas_call(cross_kernel, in_specs=[pl.BlockSpec(memory_space=pltpu.VM...]
  transfers between devices with their start and end apart: 3 -> 2, of which waited for: 2 -> 1; matrix products, arithmetic and copies ran while one was open for 1% -> 1% of each run, Pallas kernels for 1% -> 1%
where the time goes in v4:
time: 62.5 us; the launch traced here: 62.3 us
  waiting for transfers between devices  28 us (45%)
  blocking collectives  13.6 us (22%)
  starting transfers between devices  12.3 us (20%)
  Pallas kernels  6.95 us (11%)
  other arithmetic  1.21 us (2%)
    all_to_all x1, waiting for transfers between devices, shards(): arrived = lax.all_to_all(sent, EVERY, 0, 0, tiled=True)  28 us
    all_to_all x1, blocking collectives, shards(): partial = lax.all_to_all(partial, EVERY, 0, 0, tiled=True)  13.6 us
    all_to_all x1, starting transfers between devices, shards(): arrived = lax.all_to_all(sent, EVERY, 0, 0, tiled=True)  11.5 us
    pallas_call x1, Pallas kernels, half_transform(): pl.pallas_call(half_kernel, in_specs=[pl.BlockSpec(memory_space=pl.ANY)]...  3.69 us
    pallas_call x1, Pallas kernels, cross_partial(): pl.pallas_call(cross_kernel, in_specs=[pl.BlockSpec(memory_space=pltpu.VM...  2.37 us
  transfers between devices with their start and end apart: 2, of which 1 were waited for; matrix products, arithmetic and copies ran while one was open for 1% of the time, Pallas kernels for 1%

profile of v4, /device:TPU:1, one launch (start us, length us, event | category | flops | bytes accessed | tf_op | source)
XLA Modules:
  0.0 62.3 jit_solution(12815143673441977349)
XLA Ops:
  0.0 3.7 %shard_map.100 = bf16[4,32,16,512]{3,2,1,0:T(8,128)(2,1)} custom-call(bf16[256,2048]{1,0:T(8,128)(2,1)} %bitcast.7, bf16[256,2048]{1,0:T(8,128)(2,1)} %bitcast.8, bf16[2048,256]{1,0:T(8,128)(2,1)} %constant.14.clone.table_hbm), custom_call_target="tpu_custom_call" | custom-call | flops 536870912 | bytes 5242880 | tf_op jit(solution)/shard_map/pallas_call | solution.py:160
  3.7 0.0 copy-start
  3.7 0.0 copy-start.4
  3.7 0.0 copy-start.5
  3.7 0.0 copy-start.6
  3.7 11.5 %all-to-all-start = ((bf16[128,16,512]{2,1,0:T(8,128)(2,1)}), bf16[128,16,512]{2,1,0:T(8,128)(2,1)S(1)}, u32[]{:S(2)}, u32[]{:S(2)}) async-start(bf16[128,16,512]{2,1,0:T(8,128)(2,1)} %bitcast.6), calls=%async_computation | async-start | bytes 4194304 | tf_op jit(solution)/shard_map/all_to_all | solution.py:350
  15.3 0.0 copy-done
  15.3 0.0 copy-start.1
  15.3 0.0 copy-start.2
  15.3 0.0 copy-start.3
  15.3 0.8 %collective-permute-start = (f32[1,2048]{1,0:T(1,128)S(1)}, f32[1,2048]{1,0:T(1,128)S(1)}, u32[]{:S(2)}, u32[]{:S(2)}) collective-permute-start(f32[1,2048]{1,0:T(1,128)S(1)} %slice.14), channel_id=1, source_target_pairs={{64,0},{65,1},{66,2},{67,3}} | collective-permute-start | bytes 24584 | tf_op jit(solution)/shard_map/ppermute | solution.py:351
  16.1 0.0 copy-done.4
  16.1 0.2 select_reduce_fusion.1
  16.3 0.2 select_reduce_fusion
  16.5 0.1 multiply_divide_fusion
  16.6 0.0 collective-permute-done.nyquist_ref
  16.6 0.9 %shard_map.101 = (f32[4,16,256]{2,1,0:T(8,128)S(1)}, f32[16,128]{1,0:T(8,128)S(1)}) custom-call(f32[64,2048]{1,0:T(8,128)S(1)} %copy-done, f32[1,2048]{1,0:T(1,128)S(1)} %collective-permute-done.nyquist_ref), custom_call_target="tpu_custom_call" | custom-call | flops 1000000000 | bytes 1048576 | tf_op jit(solution)/shard_map/pallas_call | solution.py:223
  17.5 28.0 %all-to-all-done = bf16[128,16,512]{2,1,0:T(8,128)(2,1)S(1)} async-done(((bf16[128,16,512]{2,1,0:T(8,128)(2,1)}), bf16[128,16,512]{2,1,0:T(8,128)(2,1)S(1)}, u32[]{:S(2)}, u32[]{:S(2)}) %all-to-all-start) | async-done | bytes 2097184 | tf_op jit(solution)/shard_map/all_to_all | solution.py:350
  45.5 0.0 copy-done.1
  45.5 2.4 %shard_map.102 = f32[128,1,128]{2,1,0:T(1,128)S(1)} custom-call(bf16[4,32,16,512]{3,2,1,0:T(8,128)(2,1)S(1)} %bitcast.5, bf16[2,256,256]{2,1,0:T(8,128)(2,1)S(1)} %copy-done.1, f32[2,32,128]{2,1,0:T(8,128)S(1)} %copy-done.3, bf16[256,256]{1,0:T(8,128)(2,1)S(1)} %copy-done.2, f32[4,16,256]{2,1,0:T(8,128)S(1)} %get-tuple-element.9.weight_ref, ...), custom_call_target="tpu_custom_call" | custom-call | flops 3000000000 | bytes 5242880 | tf_op jit(solution)/shard_map/pallas_call | solution.py:324
  47.9 13.6 %all_to_all.10 = f32[128,1,128]{2,1,0:T(1,128)S(1)} all-to-all(f32[128,1,128]{2,1,0:T(1,128)S(1)} %shard_map.102), channel_id=1, replica_groups=mesh['grid'=32,'row'=4] {'row','grid'}, dimensions={0} | all-to-all | bytes 131072 | tf_op jit(solution)/shard_map/all_to_all | solution.py:357
  61.5 0.2 reduce_sum.29
  61.6 0.1 reshape.35
  61.7 0.6 mul.28
  (6 shorter events, 0.0 us)
Async XLA Ops:
  3.7 11.6 %copy-start = (f32[64,2048]{1,0:T(8,128)S(1)}, f32[64,2048]{1,0:T(8,128)}, u32[]{:S(2)}) copy-start(f32[64,2048]{1,0:T(8,128)} %spectrum_ref.1) | copy-start | bytes 1572868
  3.7 12.4 %copy-start.4 = (f32[2048]{0:T(1024)S(1)}, f32[2048]{0:T(1024)}, u32[]{:S(2)}) copy-start(f32[2048]{0:T(1024)} %param.15) | copy-start | bytes 24580
  3.7 12.4 %copy-start.5 = (s32[4]{0:T(128)S(1)}, s32[4]{0:T(128)}, u32[]{:S(2)}) copy-start(s32[4]{0:T(128)} %param.13) | copy-start | bytes 52
  3.7 12.6 %copy-start.6 = (s32[16]{0:T(128)S(1)}, s32[16]{0:T(128)}, u32[]{:S(2)}) copy-start(s32[16]{0:T(128)} %param.14) | copy-start | bytes 196
  3.7 41.8 %all-to-all-start = ((bf16[128,16,512]{2,1,0:T(8,128)(2,1)}), bf16[128,16,512]{2,1,0:T(8,128)(2,1)S(1)}, u32[]{:S(2)}, u32[]{:S(2)}) async-start(bf16[128,16,512]{2,1,0:T(8,128)(2,1)} %bitcast.6), calls=%async_computation | async-start | bytes 4194304 | tf_op jit(solution)/shard_map/all_to_all | solution.py:350
  15.3 30.2 %copy-start.1 = (bf16[2,256,256]{2,1,0:T(8,128)(2,1)S(1)}, bf16[2,256,256]{2,1,0:T(8,128)(2,1)}, u32[]{:S(2)}) copy-start(bf16[2,256,256]{2,1,0:T(8,128)(2,1)} %constant.15.clone.outer_ref) | copy-start | bytes 786436
  15.3 30.2 %copy-start.2 = (bf16[256,256]{1,0:T(8,128)(2,1)S(1)}, bf16[256,256]{1,0:T(8,128)(2,1)}, u32[]{:S(2)}) copy-start(bf16[256,256]{1,0:T(8,128)(2,1)} %constant.17.clone.inner_ref) | copy-start | bytes 393220
  15.3 30.2 %copy-start.3 = (f32[2,32,128]{2,1,0:T(8,128)S(1)}, f32[2,32,128]{2,1,0:T(8,128)}, u32[]{:S(2)}) copy-start(f32[2,32,128]{2,1,0:T(8,128)} %constant.16.clone.twist_ref) | copy-start | bytes 98308
  15.3 1.3 %collective-permute-start = (f32[1,2048]{1,0:T(1,128)S(1)}, f32[1,2048]{1,0:T(1,128)S(1)}, u32[]{:S(2)}, u32[]{:S(2)}) collective-permute-start(f32[1,2048]{1,0:T(1,128)S(1)} %slice.14), channel_id=1, source_target_pairs={{64,0},{65,1},{66,2},{67,3}} | collective-permute-start | bytes 24584 | tf_op jit(solution)/shard_map/ppermute | solution.py:351

commit v5 on v4

--- a/solution.py
+++ b/solution.py
@@ -118,9 +118,9 @@
     ]
     tables = [
         pltpu.make_async_copy(
-            table_hbm.at[pl.ds(N // 2 * k, N // 2)], table_ref.at[pl.ds(N // 2 * k, N // 2)], table_sem.at[k]
+            table_hbm.at[pl.ds(LANES * k, LANES)], table_ref.at[pl.ds(LANES * k, LANES)], table_sem.at[k]
         )
-        for k in range(2)
+        for k in range(KINDS)
     ]
     for copy in blocks[0] + blocks[1] + tables:
         copy.start()
@@ -141,8 +141,7 @@
             lax.fori_loop(0, rows // 16, fold_rows, 0, unroll=True)
     sends = []
     for kind in range(KINDS):
-        if kind % 4 == 0:
-            tables[kind // 4].wait()
+        tables[kind].wait()
         value = lax.dot_general(
             table_ref[pl.ds(LANES * kind, LANES), :], fold_ref[kind], NT, preferred_element_type=jnp.float32
         )
@@ -168,7 +167,7 @@
             pltpu.VMEM((KINDS, 2 * LANES, N // 8), jnp.bfloat16),
             pltpu.VMEM((KINDS, SLABS // 2, 16, 2 * LANES), jnp.bfloat16),
             pltpu.SemaphoreType.DMA((2, SPLIT)),
-            pltpu.SemaphoreType.DMA((2,)),
+            pltpu.SemaphoreType.DMA((KINDS,)),
             pltpu.SemaphoreType.DMA((KINDS,)),
         ],
         compiler_params=pltpu.CompilerParams(vmem_limit_bytes=60 * 2**20),

time: 62.5 us -> 63.7 us (1.019)
  Pallas kernels: 6.95 us -> 8.18 us
    pallas_call x1, Pallas kernels: 3.69 us -> 4.92 us  [half_transform(): pl.pallas_call(half_kernel, in_specs=[pl.BlockSpec(memory_space=pl.ANY)]...]
where the time goes in v5:
time: 63.7 us; the launch traced here: 63.5 us
  waiting for transfers between devices  28 us (44%)
  blocking collectives  13.6 us (21%)
  starting transfers between devices  12.3 us (19%)
  Pallas kernels  8.18 us (13%)
  other arithmetic  1.21 us (2%)
    all_to_all x1, waiting for transfers between devices, shards(): arrived = lax.all_to_all(sent, EVERY, 0, 0, tiled=True)  28 us
    all_to_all x1, blocking collectives, shards(): partial = lax.all_to_all(partial, EVERY, 0, 0, tiled=True)  13.6 us
    all_to_all x1, starting transfers between devices, shards(): arrived = lax.all_to_all(sent, EVERY, 0, 0, tiled=True)  11.5 us
    pallas_call x1, Pallas kernels, half_transform(): pl.pallas_call(half_kernel, in_specs=[pl.BlockSpec(memory_space=pl.ANY)]...  4.92 us
    pallas_call x1, Pallas kernels, cross_partial(): pl.pallas_call(cross_kernel, in_specs=[pl.BlockSpec(memory_space=pltpu.VM...  2.37 us
  transfers between devices with their start and end apart: 2, of which 1 were waited for; matrix products, arithmetic and copies ran while one was open for 1% of the time, Pallas kernels for 1%

profile of v5, /device:TPU:1, one launch (start us, length us, event | category | flops | bytes accessed | tf_op | source)
XLA Modules:
  0.0 63.5 jit_solution(295298130192346793)
XLA Ops:
  0.0 4.9 %shard_map.100 = bf16[4,32,16,512]{3,2,1,0:T(8,128)(2,1)} custom-call(bf16[256,2048]{1,0:T(8,128)(2,1)} %bitcast.7, bf16[256,2048]{1,0:T(8,128)(2,1)} %bitcast.8, bf16[2048,256]{1,0:T(8,128)(2,1)} %constant.14.clone.table_hbm), custom_call_target="tpu_custom_call" | custom-call | flops 536870912 | bytes 5242880 | tf_op jit(solution)/shard_map/pallas_call | solution.py:159
  4.9 0.0 copy-start
  4.9 0.0 copy-start.4
  5.0 0.0 copy-start.5
  5.0 0.0 copy-start.6
  5.0 11.5 %all-to-all-start = ((bf16[128,16,512]{2,1,0:T(8,128)(2,1)}), bf16[128,16,512]{2,1,0:T(8,128)(2,1)S(1)}, u32[]{:S(2)}, u32[]{:S(2)}) async-start(bf16[128,16,512]{2,1,0:T(8,128)(2,1)} %bitcast.6), calls=%async_computation | async-start | bytes 4194304 | tf_op jit(solution)/shard_map/all_to_all | solution.py:349
  16.5 0.0 copy-done
  16.5 0.0 copy-start.1
  16.5 0.0 copy-start.2
  16.5 0.0 copy-start.3
  16.5 0.8 %collective-permute-start = (f32[1,2048]{1,0:T(1,128)S(1)}, f32[1,2048]{1,0:T(1,128)S(1)}, u32[]{:S(2)}, u32[]{:S(2)}) collective-permute-start(f32[1,2048]{1,0:T(1,128)S(1)} %slice.14), channel_id=1, source_target_pairs={{64,0},{65,1},{66,2},{67,3}} | collective-permute-start | bytes 24584 | tf_op jit(solution)/shard_map/ppermute | solution.py:350
  17.3 0.0 copy-done.4
  17.4 0.0 copy-done.5
  17.4 0.2 select_reduce_fusion.1
  17.6 0.2 select_reduce_fusion
  17.8 0.1 multiply_divide_fusion
  17.8 0.0 collective-permute-done.nyquist_ref
  17.8 0.9 %shard_map.101 = (f32[4,16,256]{2,1,0:T(8,128)S(1)}, f32[16,128]{1,0:T(8,128)S(1)}) custom-call(f32[64,2048]{1,0:T(8,128)S(1)} %copy-done, f32[1,2048]{1,0:T(1,128)S(1)} %collective-permute-done.nyquist_ref), custom_call_target="tpu_custom_call" | custom-call | flops 1000000000 | bytes 1048576 | tf_op jit(solution)/shard_map/pallas_call | solution.py:222
  18.7 28.0 %all-to-all-done = bf16[128,16,512]{2,1,0:T(8,128)(2,1)S(1)} async-done(((bf16[128,16,512]{2,1,0:T(8,128)(2,1)}), bf16[128,16,512]{2,1,0:T(8,128)(2,1)S(1)}, u32[]{:S(2)}, u32[]{:S(2)}) %all-to-all-start) | async-done | bytes 2097184 | tf_op jit(solution)/shard_map/all_to_all | solution.py:349
  46.7 2.4 %shard_map.102 = f32[128,1,128]{2,1,0:T(1,128)S(1)} custom-call(bf16[4,32,16,512]{3,2,1,0:T(8,128)(2,1)S(1)} %bitcast.5, bf16[2,256,256]{2,1,0:T(8,128)(2,1)S(1)} %copy-done.1, f32[2,32,128]{2,1,0:T(8,128)S(1)} %copy-done.3, bf16[256,256]{1,0:T(8,128)(2,1)S(1)} %copy-done.2, f32[4,16,256]{2,1,0:T(8,128)S(1)} %get-tuple-element.9.weight_ref, ...), custom_call_target="tpu_custom_call" | custom-call | flops 3000000000 | bytes 5242880 | tf_op jit(solution)/shard_map/pallas_call | solution.py:323
  49.1 13.6 %all_to_all.10 = f32[128,1,128]{2,1,0:T(1,128)S(1)} all-to-all(f32[128,1,128]{2,1,0:T(1,128)S(1)} %shard_map.102), channel_id=1, replica_groups=mesh['grid'=32,'row'=4] {'row','grid'}, dimensions={0} | all-to-all | bytes 131072 | tf_op jit(solution)/shard_map/all_to_all | solution.py:356
  62.7 0.2 reduce_sum.29
  62.8 0.1 reshape.35
  62.9 0.6 mul.28
  (6 shorter events, 0.0 us)
Async XLA Ops:
  4.9 11.6 %copy-start = (f32[64,2048]{1,0:T(8,128)S(1)}, f32[64,2048]{1,0:T(8,128)}, u32[]{:S(2)}) copy-start(f32[64,2048]{1,0:T(8,128)} %spectrum_ref.1) | copy-start | bytes 1572868
  4.9 12.4 %copy-start.4 = (f32[2048]{0:T(1024)S(1)}, f32[2048]{0:T(1024)}, u32[]{:S(2)}) copy-start(f32[2048]{0:T(1024)} %param.15) | copy-start | bytes 24580
  5.0 12.4 %copy-start.5 = (s32[4]{0:T(128)S(1)}, s32[4]{0:T(128)}, u32[]{:S(2)}) copy-start(s32[4]{0:T(128)} %param.13) | copy-start | bytes 52
  5.0 12.6 %copy-start.6 = (s32[16]{0:T(128)S(1)}, s32[16]{0:T(128)}, u32[]{:S(2)}) copy-start(s32[16]{0:T(128)} %param.14) | copy-start | bytes 196
  5.0 41.7 %all-to-all-start = ((bf16[128,16,512]{2,1,0:T(8,128)(2,1)}), bf16[128,16,512]{2,1,0:T(8,128)(2,1)S(1)}, u32[]{:S(2)}, u32[]{:S(2)}) async-start(bf16[128,16,512]{2,1,0:T(8,128)(2,1)} %bitcast.6), calls=%async_computation | async-start | bytes 4194304 | tf_op jit(solution)/shard_map/all_to_all | solution.py:349
  16.5 30.2 %copy-start.1 = (bf16[2,256,256]{2,1,0:T(8,128)(2,1)S(1)}, bf16[2,256,256]{2,1,0:T(8,128)(2,1)}, u32[]{:S(2)}) copy-start(bf16[2,256,256]{2,1,0:T(8,128)(2,1)} %constant.15.clone.outer_ref) | copy-start | bytes 786436
  16.5 30.2 %copy-start.2 = (bf16[256,256]{1,0:T(8,128)(2,1)S(1)}, bf16[256,256]{1,0:T(8,128)(2,1)}, u32[]{:S(2)}) copy-start(bf16[256,256]{1,0:T(8,128)(2,1)} %constant.17.clone.inner_ref) | copy-start | bytes 393220
  16.5 30.2 %copy-start.3 = (f32[2,32,128]{2,1,0:T(8,128)S(1)}, f32[2,32,128]{2,1,0:T(8,128)}, u32[]{:S(2)}) copy-start(f32[2,32,128]{2,1,0:T(8,128)} %constant.16.clone.twist_ref) | copy-start | bytes 98308
  16.5 1.3 %collective-permute-start = (f32[1,2048]{1,0:T(1,128)S(1)}, f32[1,2048]{1,0:T(1,128)S(1)}, u32[]{:S(2)}, u32[]{:S(2)}) collective-permute-start(f32[1,2048]{1,0:T(1,128)S(1)} %slice.14), channel_id=1, source_target_pairs={{64,0},{65,1},{66,2},{67,3}} | collective-permute-start | bytes 24584 | tf_op jit(solution)/shard_map/ppermute | solution.py:350
